TPU v7x, 128 devices: a whole 4x4x4 slice. The times are simulated.
128 devices in a mesh: grid: 4 (over x), blk: 32 (over z, y, core).
Axes of the slice: x: 4, y: 4, z: 4, core: 2. Of those that a mesh axis runs over, the one named last changes fastest.
Arguments:
- state: float32 [4, 4, 128, 128, 128], P('grid', None, 'blk'), may hold values from -6 to 6
- metric: float32 [4, 9, 128, 128, 128], P('grid', None, 'blk'), may hold values from -3 to 3
- damping: float32 [4, 128, 128, 128], P('grid', 'blk'), may hold values from 0 to 1.5
- donor: int32 [4, 131072], P('grid', 'blk'), may hold values from 16384 to 81790, as said below
- fractions: float32 [4, 3, 131072], P('grid', None, 'blk'), may hold values from 0 to 1
- dest: int32 [4, 131072, 1], P('grid', 'blk'), may hold values from 0 to 127; in each aligned block of 4096 rows (0 to 4095, 4096 to 8191, ..., all dimensions but the last counted through in order) at most 64 rows name the same one
- recept: int32 [4, 131072], P('grid', 'blk'), may hold values from 0 to 65535
Outputs:
- updated: float32 [4, 4, 128, 128, 128], P('grid', None, 'blk')
Inputs may be any that keep to these rules, and one draw needn't show every extreme that they name: A flat index a * 128 * 128 + c * 128 + e into the donor's block extended by one cell at both ends of the first dimension, with a from 1 to 4 (to 3 on the last block of each grid), c below 127 and e below 127. `dest`: among the rows of one device, at most 64 name the same receiving block. `recept`: a cell of the receiving block, flat over its three dimensions.
All inputs are finite; a program needn't handle non-finite values.
Results may differ from a plain program's by a relative error of at most 0.00002.
Values sent between devices are 32-bit elements; how exact they have to be, the bound alone decides.
No kernel may reach another device: no remote copies, remote signals or barrier semaphores. Data moves between devices by JAX's collectives and lax.ppermute only.
A program may use at most 192 MiB of HBM per device.

v0:
```python
import jax
import jax.numpy as jnp
from jax import lax
from jax.sharding import PartitionSpec as P

step_size = 0.4
penalty = 1.0


def padded_2(block, sides, width):
    for axis, dim in sides:
        count = lax.axis_size(axis)
        forward = [(i, i + 1) for i in range(count - 1)]
        backward = [(target, source) for source, target in forward]
        low = lax.ppermute(
            lax.slice_in_dim(block, block.shape[dim] - width, None, axis=dim), axis, forward
        )
        high = lax.ppermute(lax.slice_in_dim(block, 0, width, axis=dim), axis, backward)
        block = jnp.concatenate([low, block, high], axis=dim)
    return block


def tendency(extended, metric, damping, fringe_sum, fringe_count):
    padded = jnp.pad(extended, ((0, 0), (0, 0), (1, 1), (1, 1)))
    interior = extended[:, 1:-1]
    differences = (
        (padded[:, 2:, 1:-1, 1:-1] - padded[:, :-2, 1:-1, 1:-1]) * 0.5,
        (padded[:, 1:-1, 2:, 1:-1] - padded[:, 1:-1, :-2, 1:-1]) * 0.5,
        (padded[:, 1:-1, 1:-1, 2:] - padded[:, 1:-1, 1:-1, :-2]) * 0.5,
    )

    def gradient(component, direction):
        return (
            metric[direction] * differences[0][component]
            + metric[3 + direction] * differences[1][component]
            + metric[6 + direction] * differences[2][component]
        )

    pressure = -(gradient(1, 0) + gradient(2, 1) + gradient(3, 2))
    fluxes = jnp.stack([pressure, -gradient(0, 0), -gradient(0, 1), -gradient(0, 2)])
    return (
        fluxes - damping[None] * interior + penalty * (fringe_sum - fringe_count[None] * interior)
    )


def corner_tables(extended_shape, base_index, fractions):
    plane_size = extended_shape[2] * extended_shape[3]
    line_size = extended_shape[3]
    offsets = []
    weights = []
    for shift_x in (0, 1):
        weight_x = fractions[0] if shift_x else 1.0 - fractions[0]
        for shift_y in (0, 1):
            weight_y = fractions[1] if shift_y else 1.0 - fractions[1]
            for shift_z in (0, 1):
                weight_z = fractions[2] if shift_z else 1.0 - fractions[2]
                offsets.append(base_index + shift_x * plane_size + shift_y * line_size + shift_z)
                weights.append(weight_x * weight_y * weight_z)
    return (jnp.stack(offsets).reshape(-1), jnp.stack(weights))


def interpolate(extended, corner_index, corner_weight):
    flattened = extended.reshape(extended.shape[0], -1)
    corners = jnp.take(flattened, corner_index, axis=1).reshape(extended.shape[0], 8, -1)
    accumulated = jnp.zeros((extended.shape[0], corner_weight.shape[1]), jnp.float32)
    for corner_number in range(8):
        accumulated = accumulated + corner_weight[corner_number][None] * corners[:, corner_number]
    return accumulated


def slot_ranks(target, device_count):
    lanes = jnp.arange(device_count, dtype=jnp.int32)
    member = (target[:, None] == lanes[None, :]).astype(jnp.int32)
    earlier = jnp.cumsum(member, axis=0) - member
    return jnp.sum(earlier * member, axis=1)


def send_fringe(outgoing, labels):
    if labels is None:
        return (
            lax.all_to_all(outgoing, ("grid", "blk"), split_axis=1, concat_axis=1, tiled=True),
            None,
        )
    arrived, arrived_labels = (
        lax.all_to_all(outgoing, ("grid", "blk"), split_axis=1, concat_axis=1, tiled=True),
        lax.all_to_all(labels, ("grid", "blk"), split_axis=1, concat_axis=1, tiled=True),
    )
    return (arrived, arrived_labels)


def local(state, metric, damping, donor, fractions, dest, recept):
    grid_count = lax.axis_size("grid")
    block_count = lax.axis_size("blk")
    device_count = grid_count * block_count
    current = state[0]
    metric_block = metric[0]
    damping_block = damping[0]
    donor_rows = donor[0]
    fraction_rows = fractions[0]
    target = dest[0, :, 0]
    receptor = recept[0]
    row_count = donor_rows.shape[0]
    capacity = 2 * row_count // device_count
    block_shape = current.shape[1:]
    cell_count = block_shape[0] * block_shape[1] * block_shape[2]
    slot_count = device_count * capacity
    positions = target * capacity + slot_ranks(target, device_count)
    labels = jnp.full((1, slot_count), cell_count, jnp.int32).at[0, positions].set(receptor)
    source = (
        jnp.zeros((slot_count,), jnp.int32)
        .at[positions]
        .set(jnp.arange(row_count, dtype=jnp.int32) + 1)
    )
    extended_shape = (4, block_shape[0] + 2, block_shape[1], block_shape[2])
    corner_index, corner_weight = corner_tables(extended_shape, donor_rows, fraction_rows)

    def extend(values_now):
        return padded_2(values_now, (("blk", 1),), 1)

    def pack(extended):
        interpolated = interpolate(extended, corner_index, corner_weight)
        padded_rows = jnp.concatenate([jnp.zeros((4, 1), jnp.float32), interpolated], axis=1)
        return jnp.take(padded_rows, source, axis=1)

    def deposit(incoming, received):
        summed = jnp.zeros((4, cell_count), jnp.float32).at[:, received].add(incoming, mode="drop")
        return summed.reshape((4,) + block_shape)

    extended = extend(current)
    incoming, received = send_fringe(pack(extended), labels)
    received = received[0]
    arrivals = jnp.zeros((cell_count,), jnp.float32).at[received].add(1.0, mode="drop")
    arrivals = arrivals.reshape(block_shape)
    first_rate = tendency(
        extended, metric_block, damping_block, deposit(incoming, received), arrivals
    )
    section = current + step_size * first_rate
    extended = extend(section)
    incoming, unused_labels = send_fringe(pack(extended), None)
    second_rate = tendency(
        extended, metric_block, damping_block, deposit(incoming, received), arrivals
    )
    updated = current + 0.5 * step_size * (first_rate + second_rate)
    return updated[None]


def solution(mesh):
    in_specs = (
        P("grid", None, "blk", None, None),
        P("grid", None, "blk", None, None),
        P("grid", "blk", None, None),
        P("grid", "blk"),
        P("grid", None, "blk"),
        P("grid", "blk", None),
        P("grid", "blk"),
    )
    out_specs = P("grid", None, "blk", None, None)
    return jax.shard_map(local, mesh=mesh, in_specs=in_specs, out_specs=out_specs, check_vma=False)
```

profile of v0, /device:TPU:1, one launch (start us, length us, event | category | flops | bytes accessed | tf_op | source)
XLA Modules:
  0.0 775.6 jit_solution(1553784571019633503)
XLA Ops:
  0.0 1.9 fusion.112
  1.9 4.6 collective-permute-start.1
  6.5 1.9 collective-permute-start
  10.1 1.2 copy.32
  11.4 1.4 fusion.35
  13.2 15.7 %scatter_custom_fusion.4 = s32[8192]{0:T(1024)S(1)} fusion(s32[4096]{0:T(1024)S(1)} %broadcast_select_fusion.4, s32[4096]{0:T(1024)} %bitcast.338, s32[]{:T(128)} %constant.34.clone.1), kind=kCustom, calls=%fused_computation.200 | custom fusion | bytes 33280
  29.6 10.5 %all-to-all-start = ((s32[1,128,64]{2,0,1:T(1,128)}), s32[1,128,64]{2,0,1:T(1,128)S(1)}, u32[]{:S(2)}, u32[]{:S(2)}) async-start(s32[1,128,64]{2,0,1:T(1,128)} %bitcast.23), calls=%async_computation | async-start | bytes 131072 | tf_op jit(solution)/shard_map/all_to_all | solution.py:86
  40.6 15.5 %scatter_custom_fusion = s32[8192]{0:T(1024)S(1)} fusion(s32[4096]{0:T(1024)S(1)} %bitcast.330, s32[4096]{0:T(1024)S(1)} %iota_add_fusion, s32[]{:T(128)} %constant.36.clone.1), kind=kCustom, calls=%fused_computation.203 | custom fusion | bytes 32772 | tf_op jit(solution)/shard_map/scatter | solution.py:112
  58.9 44.3 %scatter_custom_fusion.2 = f32[65536]{0:T(1024)} fusion(s32[8192]{0:T(1024)S(1)} %bitcast.335, f32[8192]{0:T(1024)S(1)} %broadcast.181, f32[]{:T(128)} %constant.33.clone.1), kind=kCustom, calls=%fused_computation.187 | custom fusion | flops 8192 | bytes 262148 | tf_op jit(solution)/shard_map/scatter-add | solution.py:132
  104.5 24.7 %copy.34 = f32[4,6,128,128]{0,3,2,1:T(8,128)} copy(f32[4,6,128,128]{3,2,1,0:T(8,128)S(1)} %pad_maximum_fusion) | data formatting | bytes 3145728 | tf_op jit(solution)/shard_map/concatenate | solution.py:19
  129.2 123.9 %gather_fusion = f32[32768,4]{1,0:T(8,128)} fusion(f32[4,98304]{0,1:T(8,128)} %bitcast.305, s32[32768]{0:T(1024)S(1)} %fusion.101), kind=kCustom, calls=%fused_computation.clone | custom fusion | bytes 1179648 | tf_op jit(solution)/shard_map/jit(_take)/gather | solution.py:64
  253.1 17.9 %broadcast_select_fusion.1 = f32[32768,4]{1,0:T(8,128)S(1)} fusion(f32[32768,4]{1,0:T(8,128)} %gather_fusion, pred[32768]{0:T(1024)(128)(4,1)S(1)} %compare_and_fusion), kind=kLoop, calls=%fused_computation.14 | loop fusion | flops 131072 | bytes 1081344 | tf_op jit(solution)/shard_map/jit(_take)/select_n | solution.py:64
  271.1 5.2 fusion.20
  277.0 27.8 %gather_fusion.1 = f32[8192,4]{1,0:T(8,128)} fusion(f32[4,4097]{0,1:T(8,128)S(1)} %concatenate.33, s32[8192]{0:T(1024)S(1)} %copy-done.11), kind=kCustom, calls=%fused_computation.1.clone | custom fusion | bytes 294912 | tf_op jit(solution)/shard_map/jit(_take)/gather | solution.py:123
  304.8 7.5 broadcast_select_fusion.3
  312.3 3.0 copy.35
  316.2 10.2 %all-to-all-start.1 = ((f32[128,1,256]{2,1,0:T(1,128)}), f32[128,1,256]{2,1,0:T(1,128)}, u32[]{:S(2)}, u32[]{:S(2)}) async-start(f32[128,1,256]{2,1,0:T(1,128)} %reshape.397), calls=%async_computation.1 | async-start | bytes 262144 | tf_op jit(solution)/shard_map/all_to_all | solution.py:85
  326.4 3.6 fusion.39
  332.2 3.9 all-to-all-done.1
  336.7 2.6 reduce.8
  339.2 1.8 reshape.398
  341.0 1.7 copy.36
  342.7 1.7 reshape.337
  344.4 3.5 copy.37
  347.9 57.6 %scatter_custom_fusion.1 = f32[4,65536]{0,1:T(8,128)} fusion(s32[8192]{0:T(1024)} %bitcast.336, f32[8192,4]{1,0:T(8,128)} %copy.37, f32[]{:T(128)} %constant.33.clone.1), kind=kCustom, calls=%fused_computation.11 | custom fusion | flops 32768 | bytes 1049088 | tf_op jit(solution)/shard_map/scatter-add | solution.py:126
  405.6 20.3 %copy.39 = f32[4,4,128,128]{3,2,1,0:T(8,128)} copy(f32[4,4,128,128]{0,3,2,1:T(8,128)} %bitcast.299) | data formatting | bytes 2097152 | tf_op jit(solution)/shard_map/reshape | solution.py:127
  425.8 2.0 fusion.53
  429.6 2.9 collective-permute-start.3
  432.5 2.1 collective-permute-start.2
  434.7 20.3 %copy.38 = f32[1,4,4,128,128]{4,3,2,1,0:T(8,128)} copy(f32[1,4,4,128,128]{1,4,3,2,0:T(8,128)} %bitcast.300) | data formatting | bytes 2097152 | tf_op jit(solution)/shard_map/reshape | solution.py:127
  454.9 1.4 pad_maximum_fusion.1
  457.5 2.0 fusion.43
  459.5 25.7 %copy.40 = f32[4,6,128,128]{0,3,2,1:T(8,128)} copy(f32[4,6,128,128]{3,2,1,0:T(8,128)} %copy-done.2) | data formatting | bytes 3145728 | tf_op jit(solution)/shard_map/concatenate | solution.py:19
  485.2 123.9 %gather_fusion.2 = f32[32768,4]{1,0:T(8,128)} fusion(f32[4,98304]{0,1:T(8,128)} %bitcast.304, s32[32768]{0:T(1024)S(1)} %fusion.101), kind=kCustom, calls=%fused_computation.2.clone | custom fusion | bytes 1179648 | tf_op jit(solution)/shard_map/jit(_take)/gather | solution.py:64
  609.1 16.2 %broadcast_select_fusion = f32[32768,4]{1,0:T(8,128)S(1)} fusion(f32[32768,4]{1,0:T(8,128)} %gather_fusion.2, pred[32768]{0:T(1024)(128)(4,1)} %copy-done.10), kind=kLoop, calls=%fused_computation.13 | loop fusion | flops 131072 | bytes 1081344 | tf_op jit(solution)/shard_map/jit(_take)/select_n | solution.py:64
  625.4 5.2 fusion.5
  630.6 1.6 concatenate.37
  632.2 29.3 %gather_fusion.3 = f32[8192,4]{1,0:T(8,128)} fusion(f32[4,4097]{0,1:T(8,128)} %concatenate.37, s32[8192]{0:T(1024)S(1)} %copy-done.12), kind=kCustom, calls=%fused_computation.3.clone | custom fusion | bytes 294912 | tf_op jit(solution)/shard_map/jit(_take)/gather | solution.py:123
  661.5 7.5 broadcast_select_fusion.2
  669.0 3.6 copy.41
  672.6 1.8 reshape.399
  674.5 6.7 all-to-all-start.2
  681.2 1.8 fusion.47
  685.5 5.6 all-to-all-done.2
  692.4 2.7 copy.43
  695.2 57.5 %scatter_custom_fusion.3 = f32[4,65536]{0,1:T(8,128)} fusion(s32[8192]{0:T(1024)} %bitcast.337, f32[8192,4]{1,0:T(8,128)} %copy.43, f32[]{:T(128)} %constant.33.clone.1), kind=kCustom, calls=%fused_computation.9 | custom fusion | flops 32768 | bytes 1049088 | tf_op jit(solution)/shard_map/scatter-add | solution.py:126
  752.6 19.6 %copy.44 = f32[1,4,4,128,128]{4,3,2,1,0:T(8,128)S(1)} copy(f32[1,4,4,128,128]{1,4,3,2,0:T(8,128)} %bitcast.301) | data formatting | bytes 2097152 | tf_op jit(solution)/shard_map/reshape | solution.py:127
  772.2 3.2 fusion.57
  (114 shorter events, 18.2 us)
Async XLA Ops:
  1.9 101.4 %collective-permute-start.1 = (f32[4,1,128,128]{3,2,1,0:T(8,128)}, f32[4,1,128,128]{3,2,1,0:T(8,128)S(1)}, u32[]{:S(2)}, u32[]{:S(2)}) collective-permute-start(f32[4,1,128,128]{3,2,1,0:T(8,128)} %get-tuple-element.19), channel_id=1, source_target_pairs={{0,1},{1,2},{2,3},{3,4},{4,5},{5,6},{6,7},{7,8},{8,9},{9,10},{10,1... | collective-permute-start | bytes 786440 | tf_op jit(solution)/shard_map/ppermute | solution.py:15
  6.5 96.8 %collective-permute-start = (f32[4,1,128,128]{3,2,1,0:T(8,128)}, f32[4,1,128,128]{3,2,1,0:T(8,128)}, u32[]{:S(2)}, u32[]{:S(2)}) collective-permute-start(f32[4,1,128,128]{3,2,1,0:T(8,128)} %get-tuple-element.20), channel_id=1, source_target_pairs={{1,0},{2,1},{3,2},{4,3},{5,4},{6,5},{7,6},{8,7},{9,8},{10,9},{11,1... | collective-permute-start | bytes 786440 | tf_op jit(solution)/shard_map/ppermute | solution.py:18
  10.1 1.3 copy-start.27
  11.4 1.6 copy-start.34
  11.4 1.7 copy-start.33
  11.4 28.8 %copy-start.30 = (s32[1,4096]{1,0:T(1,128)S(1)}, s32[1,4096]{1,0:T(1,128)}, u32[]{:S(2)}) copy-start(s32[1,4096]{1,0:T(1,128)} %param.14) | copy-start | bytes 49156
  11.4 29.2 %copy-start.31 = (f32[1,3,4096]{2,0,1:T(1,128)S(1)}, f32[1,3,4096]{2,0,1:T(1,128)}, u32[]{:S(2)}) copy-start(f32[1,3,4096]{2,0,1:T(1,128)} %param.15) | copy-start | bytes 147460
  11.4 91.9 %copy-start.1 = (f32[1,4,4,128,128]{4,3,2,1,0:T(8,128)S(1)}, f32[1,4,4,128,128]{4,3,2,1,0:T(8,128)}, u32[]{:S(2)}) copy-start(f32[1,4,4,128,128]{4,3,2,1,0:T(8,128)} %param.11) | copy-start | bytes 3145732
  29.6 27.9 %all-to-all-start = ((s32[1,128,64]{2,0,1:T(1,128)}), s32[1,128,64]{2,0,1:T(1,128)S(1)}, u32[]{:S(2)}, u32[]{:S(2)}) async-start(s32[1,128,64]{2,0,1:T(1,128)} %bitcast.23), calls=%async_computation | async-start | bytes 131072 | tf_op jit(solution)/shard_map/all_to_all | solution.py:86
  40.6 212.5 %copy-start.10 = (pred[32768]{0:T(1024)(128)(4,1)}, pred[32768]{0:T(1024)(128)(4,1)S(1)}, u32[]{:S(2)}) copy-start(pred[32768]{0:T(1024)(128)(4,1)S(1)} %compare_and_fusion) | copy-start | bytes 98308
  56.8 214.2 %copy-start.13 = (f32[4096]{0:T(1024)}, f32[4096]{0:T(1024)S(1)}, u32[]{:S(2)}) copy-start(f32[4096]{0:T(1024)S(1)} %get-tuple-element.22) | copy-start | bytes 49156
  56.8 214.2 %copy-start.15 = (f32[4096]{0:T(1024)}, f32[4096]{0:T(1024)S(1)}, u32[]{:S(2)}) copy-start(f32[4096]{0:T(1024)S(1)} %get-tuple-element.23) | copy-start | bytes 49156
  56.9 214.2 %copy-start.17 = (f32[4096]{0:T(1024)}, f32[4096]{0:T(1024)S(1)}, u32[]{:S(2)}) copy-start(f32[4096]{0:T(1024)S(1)} %get-tuple-element.24) | copy-start | bytes 49156
  56.9 214.2 %copy-start.19 = (f32[4096]{0:T(1024)}, f32[4096]{0:T(1024)S(1)}, u32[]{:S(2)}) copy-start(f32[4096]{0:T(1024)S(1)} %get-tuple-element.25) | copy-start | bytes 49156
  56.9 214.2 %copy-start.21 = (f32[4096]{0:T(1024)}, f32[4096]{0:T(1024)S(1)}, u32[]{:S(2)}) copy-start(f32[4096]{0:T(1024)S(1)} %get-tuple-element.26) | copy-start | bytes 49156
  56.9 214.2 %copy-start.23 = (f32[4096]{0:T(1024)}, f32[4096]{0:T(1024)S(1)}, u32[]{:S(2)}) copy-start(f32[4096]{0:T(1024)S(1)} %get-tuple-element.27) | copy-start | bytes 49156
  56.9 214.2 %copy-start.25 = (f32[4096]{0:T(1024)}, f32[4096]{0:T(1024)S(1)}, u32[]{:S(2)}) copy-start(f32[4096]{0:T(1024)S(1)} %get-tuple-element.28) | copy-start | bytes 49156
  58.9 70.2 %copy-start.32 = (s32[8192,1]{0,1:T(1,128)}, s32[8192,1]{0,1:T(1,128)S(1)}, u32[]{:S(2)}) copy-start(s32[8192,1]{0,1:T(1,128)S(1)} %compare_select_fusion.1) | copy-start | bytes 98308
  103.3 25.9 %copy-start.9 = (f32[4,1,128,128]{3,2,1,0:T(8,128)}, f32[4,1,128,128]{3,2,1,0:T(8,128)S(1)}, u32[]{:S(2)}) copy-start(f32[4,1,128,128]{3,2,1,0:T(8,128)S(1)} %collective-permute-done.1) | copy-start | bytes 786436
  104.5 24.7 %copy-start.3 = (f32[4,6,128,128]{3,2,1,0:T(8,128)}, f32[4,6,128,128]{3,2,1,0:T(8,128)S(1)}, u32[]{:S(2)}) copy-start(f32[4,6,128,128]{3,2,1,0:T(8,128)S(1)} %pad_maximum_fusion) | copy-start | bytes 4718596
  276.3 0.8 copy-start.11
  276.3 28.5 %copy-start.28 = (pred[8192]{0:T(1024)(128)(4,1)S(1)}, pred[8192]{0:T(1024)(128)(4,1)}, u32[]{:S(2)}) copy-start(pred[8192]{0:T(1024)(128)(4,1)} %compare_and_fusion.1) | copy-start | bytes 24580
  316.2 19.9 %all-to-all-start.1 = ((f32[128,1,256]{2,1,0:T(1,128)}), f32[128,1,256]{2,1,0:T(1,128)}, u32[]{:S(2)}, u32[]{:S(2)}) async-start(f32[128,1,256]{2,1,0:T(1,128)} %reshape.397), calls=%async_computation.1 | async-start | bytes 262144 | tf_op jit(solution)/shard_map/all_to_all | solution.py:85
  326.4 3.6 copy-start
  427.8 1.0 copy-start.4
  429.6 25.3 %collective-permute-start.3 = (f32[4,1,128,128]{3,2,1,0:T(8,128)}, f32[4,1,128,128]{3,2,1,0:T(8,128)}, u32[]{:S(2)}, u32[]{:S(2)}) collective-permute-start(f32[4,1,128,128]{3,2,1,0:T(8,128)} %get-tuple-element.17), channel_id=1, source_target_pairs={{0,1},{1,2},{2,3},{3,4},{4,5},{5,6},{6,7},{7,8},{8,9},{9,10},{10,1... | collective-permute-start | bytes 786440 | tf_op jit(solution)/shard_map/ppermute | solution.py:15
  432.5 22.4 %collective-permute-start.2 = (f32[4,1,128,128]{3,2,1,0:T(8,128)}, f32[4,1,128,128]{3,2,1,0:T(8,128)}, u32[]{:S(2)}, u32[]{:S(2)}) collective-permute-start(f32[4,1,128,128]{3,2,1,0:T(8,128)} %get-tuple-element.18), channel_id=1, source_target_pairs={{1,0},{2,1},{3,2},{4,3},{5,4},{6,5},{7,6},{8,7},{9,8},{10,9},{11,1... | collective-permute-start | bytes 786440 | tf_op jit(solution)/shard_map/ppermute | solution.py:18
  456.4 1.1 copy-start.2
  609.1 16.3 %copy-start.14 = (f32[4096]{0:T(1024)S(1)}, f32[4096]{0:T(1024)}, u32[]{:S(2)}) copy-start(f32[4096]{0:T(1024)} %copy-done.13) | copy-start | bytes 49156
  609.1 16.3 %copy-start.16 = (f32[4096]{0:T(1024)S(1)}, f32[4096]{0:T(1024)}, u32[]{:S(2)}) copy-start(f32[4096]{0:T(1024)} %copy-done.15) | copy-start | bytes 49156
  609.1 16.3 %copy-start.18 = (f32[4096]{0:T(1024)S(1)}, f32[4096]{0:T(1024)}, u32[]{:S(2)}) copy-start(f32[4096]{0:T(1024)} %copy-done.17) | copy-start | bytes 49156
  609.1 16.3 %copy-start.20 = (f32[4096]{0:T(1024)S(1)}, f32[4096]{0:T(1024)}, u32[]{:S(2)}) copy-start(f32[4096]{0:T(1024)} %copy-done.19) | copy-start | bytes 49156
  609.1 16.3 %copy-start.22 = (f32[4096]{0:T(1024)S(1)}, f32[4096]{0:T(1024)}, u32[]{:S(2)}) copy-start(f32[4096]{0:T(1024)} %copy-done.21) | copy-start | bytes 49156
  609.1 16.3 %copy-start.24 = (f32[4096]{0:T(1024)S(1)}, f32[4096]{0:T(1024)}, u32[]{:S(2)}) copy-start(f32[4096]{0:T(1024)} %copy-done.23) | copy-start | bytes 49156
  609.1 16.3 %copy-start.26 = (f32[4096]{0:T(1024)S(1)}, f32[4096]{0:T(1024)}, u32[]{:S(2)}) copy-start(f32[4096]{0:T(1024)} %copy-done.25) | copy-start | bytes 49156
  630.6 1.6 copy-start.12
  630.6 30.9 %copy-start.29 = (pred[8192]{0:T(1024)(128)(4,1)S(1)}, pred[8192]{0:T(1024)(128)(4,1)}, u32[]{:S(2)}) copy-start(pred[8192]{0:T(1024)(128)(4,1)} %compare_and_fusion.1) | copy-start | bytes 24580
  674.5 16.6 %all-to-all-start.2 = ((f32[128,1,256]{2,1,0:T(1,128)}), f32[128,1,256]{2,1,0:T(1,128)S(1)}, u32[]{:S(2)}, u32[]{:S(2)}) async-start(f32[128,1,256]{2,1,0:T(1,128)} %reshape.399), calls=%async_computation.2 | async-start | bytes 262144 | tf_op jit(solution)/shard_map/all_to_all | solution.py:81
  681.2 1.9 copy-start.6
  681.2 2.2 copy-start.7
  752.6 19.6 %copy-start.5 = (f32[1,4,4,128,128]{4,3,2,1,0:T(8,128)S(1)}, f32[1,4,4,128,128]{4,3,2,1,0:T(8,128)}, u32[]{:S(2)}) copy-start(f32[1,4,4,128,128]{4,3,2,1,0:T(8,128)} %copy.38) | copy-start | bytes 3145732
  752.6 19.6 %copy-start.8 = (f32[1,4,128,128]{3,2,1,0:T(8,128)S(1)}, f32[1,4,128,128]{3,2,1,0:T(8,128)}, u32[]{:S(2)}) copy-start(f32[1,4,128,128]{3,2,1,0:T(8,128)} %fusion.71) | copy-start | bytes 786436
where the time goes:
time: 784 us; the launch traced here: 776 us
  local copies, waits for them, and re-layouts  480 us (61%)
  other arithmetic  247 us (32%)
  starting transfers between devices  39 us (5%)
  waiting for transfers between devices  9.54 us (1%)
    gather x2, local copies, waits for them, and re-layouts, interpolate(): jnp.take(flattened, corner_index, axis=1).reshape(extended.shape[0], 8, -1)  248 us
    scatter-add x2, other arithmetic, deposit(): jnp.zeros((4, cell_count), jnp.float32).at[:, received]  115 us
    reshape x3, local copies, waits for them, and re-layouts, deposit(): return summed.reshape((4,) + block_shape)  60.1 us
    gather x2, local copies, waits for them, and re-layouts, pack(): return jnp.take(padded_rows, source, axis=1)  57.1 us
    concatenate x2, local copies, waits for them, and re-layouts, padded_2(): block = jnp.concatenate([low, block, high], axis=dim)  50.3 us
    scatter-add x1, other arithmetic, local(): jnp.zeros((cell_count,), jnp.float32).at[received].add(1.0, mode='drop')  44.3 us
    select_n x2, other arithmetic, interpolate(): jnp.take(flattened, corner_index, axis=1).reshape(extended.shape[0], 8, -1)  34.2 us
    unnamed x76, local copies, waits for them, and re-layouts  23.5 us
  transfers between devices with their start and end apart: 7, of which 2 were waited for; matrix products, arithmetic and copies ran while one was open for 15% of the time, Pallas kernels for 0%

commit v1 on v0

v1 whole, which is shorter than its diff:
```python
import functools
import jax
import jax.numpy as jnp
from jax import lax
from jax.experimental import pallas as pl
from jax.experimental.pallas import tpu as pltpu
from jax.sharding import PartitionSpec as P

step_size = 0.4
f32, bf16, i32 = jnp.float32, jnp.bfloat16, jnp.int32
VMEM_LIMIT = 48 * 1024 * 1024
NT = (((1,), (1,)), ((), ()))


def iota(shape, dim):
    return lax.broadcasted_iota(i32, shape, dim)


def two_parts(x):
    high = x.astype(bf16)
    low = (x - high.astype(f32)).astype(bf16)
    return high, low


def params():
    return pltpu.CompilerParams(vmem_limit_bytes=VMEM_LIMIT)


def pack_kernel(with_labels, state, beyond, donor, fractions, dest, *rest):
    if with_labels:
        recept, out, ranks, source, total = rest
    else:
        ranks, out, source, total = rest
    tile = 256
    tiles = donor.shape[1] // tile
    for c in range(4):
        for x in range(5):
            block = state[c, x] if x < 4 else beyond[c]
            high, low = two_parts(block)
            rows = slice(c * 128, c * 128 + 128)
            source[rows, x * 128 : x * 128 + 128] = high
            source[rows, 640 + x * 128 : 640 + x * 128 + 128] = low
            source[rows, 1280 + x * 128 : 1280 + x * 128 + 128] = high
    total[...] = jnp.zeros_like(total)
    blocks = iota((128, tile), 0)
    cells = iota((128, tile), 0)
    slots = iota((64, tile), 0)
    before = (iota((tile, tile), 0) < iota((tile, tile), 1)).astype(f32).astype(bf16)

    def step(t, counted):
        here = pl.ds(pl.multiple_of(t * tile, tile), tile)
        member = blocks == dest[:, here]
        member_f = member.astype(f32)
        member_b = member_f.astype(bf16)
        if with_labels:
            earlier = jnp.dot(member_b, before, preferred_element_type=f32) + counted
            rank = jnp.sum(member_f * earlier, axis=0, keepdims=True).astype(i32)
            ranks[:, here] = rank
            counted = counted + jnp.sum(member_f, axis=1, keepdims=True)
        else:
            rank = ranks[:, here]
        base = donor[:, here]
        plane = base >> 14
        line = (base >> 7) & 127
        point = base & 127
        fx, fy, fz = fractions[0:1, here], fractions[1:2, here], fractions[2:3, here]
        wy = jnp.where(cells == line, 1.0 - fy, jnp.where(cells == line + 1, fy, 0.0))
        wz = jnp.where(cells == point, 1.0 - fz, jnp.where(cells == point + 1, fz, 0.0))
        highs, lows = [], []
        for x in range(5):
            wx = jnp.where(plane == x + 1, 1.0 - fx, jnp.where(plane == x, fx, 0.0))
            high, low = two_parts(wx * wz)
            highs.append(high)
            lows.append(low)
        weights = jnp.concatenate(highs + highs + lows, axis=0)
        lines = jnp.dot(source[...], weights, preferred_element_type=f32)
        chosen = slots == rank
        parts = []
        values = [
            jnp.sum(lines[c * 128 : c * 128 + 128] * wy, axis=0, keepdims=True) for c in range(4)
        ]
        for which in (0, 1):
            for c in range(4):
                part = two_parts(values[c])[which].astype(f32)
                parts.append(jnp.where(chosen, part, 0.0).astype(bf16))
        if with_labels:
            label = recept[:, here] + 1
            for part in (label >> 8, label & 255):
                parts.append(jnp.where(chosen, part.astype(f32), 0.0).astype(bf16))
        packed = jnp.concatenate(parts, axis=0)
        total[...] += lax.dot_general(member_b, packed, NT, preferred_element_type=f32)
        return counted

    lax.fori_loop(0, tiles, step, jnp.zeros((128, 1), f32))
    for half in range(2):
        cut = slice(half * 128, half * 128 + 128)
        low = slice(256 + half * 128, 256 + half * 128 + 128)
        out[:, half, :] = total[:, cut] + total[:, low]
    if with_labels:
        labels = total[:, 512:640]
        lane = iota((128, 128), 1)
        labels = labels * jnp.where(lane < 64, 256.0, 1.0)
        out[:, 2, :] = labels + pltpu.roll(labels, 64, 1)
        out[:, 3, :] = jnp.zeros((128, 128), f32)


def pack(state, beyond, donor, fractions, dest, recept=None, ranks=None):
    rows = donor.shape[1]
    first = ranks is None
    out = jax.ShapeDtypeStruct((128, 4 if first else 2, 128), f32)
    scratch = [pltpu.VMEM((512, 1920), bf16), pltpu.VMEM((128, 640 if first else 512), f32)]
    if first:
        return pl.pallas_call(
            functools.partial(pack_kernel, True),
            out_shape=(out, jax.ShapeDtypeStruct((1, rows), i32)),
            scratch_shapes=scratch,
            compiler_params=params(),
        )(state, beyond, donor, fractions, dest, recept)
    return pl.pallas_call(
        functools.partial(pack_kernel, False),
        out_shape=out,
        scratch_shapes=scratch,
        compiler_params=params(),
    )(state, beyond, donor, fractions, dest, ranks)


def flux_kernel(state, below, beyond, metric, damping, out):
    row = iota((128, 128), 0)
    lane = iota((128, 128), 1)

    def step(x, _):
        def differences(c):
            here = state[c, x]
            low = jnp.where(x == 0, below[c], state[c, jnp.maximum(x - 1, 0)])
            high = jnp.where(x == 3, beyond[c], state[c, jnp.minimum(x + 1, 3)])
            up = jnp.where(row < 127, pltpu.roll(here, 127, 0), 0.0)
            down = jnp.where(row > 0, pltpu.roll(here, 1, 0), 0.0)
            right = jnp.where(lane < 127, pltpu.roll(here, 127, 1), 0.0)
            left = jnp.where(lane > 0, pltpu.roll(here, 1, 1), 0.0)
            return (high - low) * 0.5, (up - down) * 0.5, (right - left) * 0.5

        def gradient(diffs, i):
            return metric[i, x] * diffs[0] + metric[3 + i, x] * diffs[1] + metric[6 + i, x] * diffs[2]

        damp = damping[x]
        diffs = differences(0)
        for i in range(3):
            out[1 + i, x] = -gradient(diffs, i) - damp * state[1 + i, x]
        pressure = -damp * state[0, x]
        for i in range(3):
            pressure = pressure - gradient(differences(1 + i), i)
        out[0, x] = pressure
        return 0

    lax.fori_loop(0, 4, step, 0)


def flux(state, below, beyond, metric, damping):
    return pl.pallas_call(
        flux_kernel,
        out_shape=jax.ShapeDtypeStruct(state.shape, f32),
        compiler_params=params(),
        cost_estimate=pl.CostEstimate(
            flops=65536 * 80, bytes_accessed=5 * 1024 * 1024, transcendentals=0
        ),
    )(state, below, beyond, metric, damping)


def deposit_kernel(with_labels, *refs):
    if with_labels:
        arrived, now, rates, labels, counts, section, base, slots, total = refs
    else:
        arrived, now, rates, labels, counts, base, out, slots, total = refs
    lane = iota((64, 128), 1)

    def halves(j):
        first, second = arrived[0:64, j, :], arrived[64:128, j, :]
        return (
            jnp.where(lane < 64, first, pltpu.roll(second, 64, 1)),
            jnp.where(lane < 64, pltpu.roll(first, 64, 1), second),
        )

    values = halves(0) + halves(1)
    for c in range(4):
        high = values[c].astype(bf16).astype(f32)
        slots[c] = high
        slots[4 + c] = values[c] - high
    if with_labels:
        labels[...] = halves(2)[0].astype(i32) - 1
    total[...] = jnp.zeros_like(total)
    lines = iota((512, 128), 0)
    points = iota((128, 128), 0)
    chunk = 8

    def step(t, _):
        selectors, spreads = [], []
        for j in range(chunk):
            label = labels[pl.ds(t * chunk + j, 1), :]
            selectors.append((lines == (label >> 7)).astype(f32).astype(bf16))
            at = points == (label & 127)
            column = [
                jnp.where(at, slots[p, pl.ds(t * chunk + j, 1), :], 0.0).astype(bf16)
                for p in range(8)
            ]
            if with_labels:
                column.append(at.astype(f32).astype(bf16))
            spreads.append(jnp.concatenate(column, axis=0))
        selector = jnp.concatenate(selectors, axis=1)
        spread = jnp.concatenate(spreads, axis=1)
        total[...] += lax.dot_general(selector, spread, NT, preferred_element_type=f32)
        return 0

    lax.fori_loop(0, 64 // chunk, step, 0)
    for x in range(4):
        rows = slice(x * 128, x * 128 + 128)
        if with_labels:
            counts[x] = total[rows, 1024:1152]
        for c in range(4):
            fringe = total[rows, c * 128 : c * 128 + 128] + total[rows, 512 + c * 128 : 640 + c * 128]
            rate = rates[c, x] + fringe - counts[x] * now[c, x]
            if with_labels:
                section[c, x] = now[c, x] + step_size * rate
                base[c, x] = now[c, x] + (0.5 * step_size) * rate
            else:
                out[c, x] = base[c, x] + (0.5 * step_size) * rate


def deposit_first(arrived, state, rates):
    return pl.pallas_call(
        functools.partial(deposit_kernel, True),
        out_shape=(
            jax.ShapeDtypeStruct((64, 128), i32),
            jax.ShapeDtypeStruct(state.shape[1:], f32),
            jax.ShapeDtypeStruct(state.shape, f32),
            jax.ShapeDtypeStruct(state.shape, f32),
        ),
        scratch_shapes=[pltpu.VMEM((8, 64, 128), f32), pltpu.VMEM((512, 1152), f32)],
        compiler_params=params(),
    )(arrived, state, rates)


def deposit_second(arrived, section, rates, labels, counts, base):
    return pl.pallas_call(
        functools.partial(deposit_kernel, False),
        out_shape=jax.ShapeDtypeStruct(section.shape, f32),
        scratch_shapes=[pltpu.VMEM((8, 64, 128), f32), pltpu.VMEM((512, 1024), f32)],
        compiler_params=params(),
    )(arrived, section, rates, labels, counts, base)


def neighbours(values):
    count = lax.axis_size("blk")
    forward = [(i, i + 1) for i in range(count - 1)]
    backward = [(i + 1, i) for i in range(count - 1)]
    beyond = lax.ppermute(values[:, 0], "blk", backward)
    below = lax.ppermute(values[:, 3], "blk", forward)
    return below, beyond


def exchange(outgoing):
    return lax.all_to_all(outgoing, ("grid", "blk"), split_axis=0, concat_axis=0, tiled=True)


def local(state, metric, damping, donor, fractions, dest, recept):
    state, metric, damping, fractions = state[0], metric[0], damping[0], fractions[0]
    dest = dest.reshape(1, -1)
    below, beyond = neighbours(state)
    outgoing, ranks = pack(state, beyond, donor, fractions, dest, recept=recept)
    arrived = exchange(outgoing)
    rates = flux(state, below, beyond, metric, damping)
    labels, counts, section, base = deposit_first(arrived, state, rates)
    below, beyond = neighbours(section)
    arrived = exchange(pack(section, beyond, donor, fractions, dest, ranks=ranks))
    rates = flux(section, below, beyond, metric, damping)
    return deposit_second(arrived, section, rates, labels, counts, base)[None]


def solution(mesh):
    in_specs = (
        P("grid", None, "blk", None, None),
        P("grid", None, "blk", None, None),
        P("grid", "blk", None, None),
        P("grid", "blk"),
        P("grid", None, "blk"),
        P("grid", "blk", None),
        P("grid", "blk"),
    )
    out_specs = P("grid", None, "blk", None, None)
    return jax.shard_map(local, mesh=mesh, in_specs=in_specs, out_specs=out_specs, check_vma=False)
```

time: 784 us -> 126 us (0.16)
  local copies, waits for them, and re-layouts: 480 us -> 13.3 us
  other arithmetic: 247 us -> 0 us
  Pallas kernels: 0 us -> 64 us
  starting transfers between devices: 39 us -> 29.6 us
  waiting for transfers between devices: 9.54 us -> 17.8 us
    gather x4 -> x0, local copies, waits for them, and re-layouts: 305 us -> none  [the longest x2 248 us: interpolate(): jnp.take(flattened, corner_index, axis=1).reshape(extended.shape[0], 8, -1)]
    scatter-add x3 -> x0, other arithmetic: 159 us -> none  [the longest x2 115 us: deposit(): jnp.zeros((4, cell_count), jnp.float32).at[:, received]]
    pallas_call x0 -> x6, Pallas kernels: none -> 64 us  [the longest x1 19.4 us: pack(): pl.pallas_call(functools.partial(pack_kernel, True), out_shape=(out, jax....]
    reshape x3 -> x0, local copies, waits for them, and re-layouts: 60.1 us -> none  [deposit(): return summed.reshape((4,) + block_shape)]
    concatenate x4 -> x0, local copies, waits for them, and re-layouts: 52.1 us -> none  [the longest x2 50.3 us: padded_2(): block = jnp.concatenate([low, block, high], axis=dim)]
    select_n x6 -> x0, other arithmetic: 49.2 us -> none  [the longest x2 34.2 us: interpolate(): jnp.take(flattened, corner_index, axis=1).reshape(extended.shape[0], 8, -1)]
    all_to_all x11 -> x0, local copies, waits for them, and re-layouts: 18.2 us -> none  [the longest x9 17 us: send_fringe(): lax.all_to_all(outgoing, ('grid', 'blk'), split_axis=1, concat_axis=1, ti...]
    add x6 -> x0, other arithmetic: 15.6 us -> none  [the longest x2 10.4 us: interpolate(): accumulated + corner_weight[corner_number][None] * corners[:, corner_number]]
  transfers between devices with their start and end apart: 7 -> 6, of which waited for: 2 -> 4; matrix products, arithmetic and copies ran while one was open for 15% -> 1% of each run, Pallas kernels for 0% -> 31%
where the time goes in v1:
time: 126 us; the launch traced here: 125 us
  Pallas kernels  64 us (51%)
  starting transfers between devices  29.6 us (23%)
  waiting for transfers between devices  17.8 us (14%)
  local copies, waits for them, and re-layouts  13.3 us (11%)
    pallas_call x1, Pallas kernels, pack(): pl.pallas_call(functools.partial(pack_kernel, True), out_shape=(out, jax....  19.4 us
    pallas_call x1, Pallas kernels, pack(): pl.pallas_call(functools.partial(pack_kernel, False), out_shape=out, scra...  17.6 us
    all_to_all x2, starting transfers between devices, exchange(): lax.all_to_all(outgoing, ('grid', 'blk'), split_axis=0, concat_axis=0, ti...  17.6 us
    all_to_all x2, waiting for transfers between devices, exchange(): lax.all_to_all(outgoing, ('grid', 'blk'), split_axis=0, concat_axis=0, ti...  14.4 us
    pallas_call x1, Pallas kernels, deposit_first(): pl.pallas_call(functools.partial(deposit_kernel, True), out_shape=(jax.Sh...  13.2 us
    unnamed x35, local copies, waits for them, and re-layouts  12.1 us
    pallas_call x1, Pallas kernels, deposit_second(): pl.pallas_call(functools.partial(deposit_kernel, False), out_shape=jax.Sh...  11.8 us
    ppermute x2, starting transfers between devices, neighbours(): beyond = lax.ppermute(values[:, 0], 'blk', backward)  6.27 us
  transfers between devices with their start and end apart: 6, of which 4 were waited for; matrix products, arithmetic and copies ran while one was open for 1% of the time, Pallas kernels for 31%

profile of v1, /device:TPU:1, one launch (start us, length us, event | category | flops | bytes accessed | tf_op | source)
XLA Modules:
  0.0 124.9 jit_solution(5409194289367814913)
XLA Ops:
  0.0 0.0 copy-start.1
  0.0 1.2 slice_bitcast_fusion.2
  1.2 3.3 %collective-permute-start = (f32[4,128,128]{2,1,0:T(8,128)S(1)}, f32[4,128,128]{2,1,0:T(8,128)S(1)}, u32[]{:S(2)}, u32[]{:S(2)}) collective-permute-start(f32[4,128,128]{2,1,0:T(8,128)S(1)} %get-tuple-element.20), channel_id=1, source_target_pairs={{1,0},{2,1},{3,2},{4,3},{5,4},{6,5},{7,6},{8,7},{9,8},{10,9},{11,1... | collective-permute-start | bytes 786440 | tf_op jit(solution)/shard_map/ppermute | solution.py:255
  4.5 3.2 %collective-permute-start.1 = (f32[4,128,128]{2,1,0:T(8,128)S(1)}, f32[4,128,128]{2,1,0:T(8,128)S(1)}, u32[]{:S(2)}, u32[]{:S(2)}) collective-permute-start(f32[4,128,128]{2,1,0:T(8,128)S(1)} %get-tuple-element.19), channel_id=1, source_target_pairs={{0,1},{1,2},{2,3},{3,4},{4,5},{5,6},{6,7},{7,8},{8,9},{9,10},{10,1... | collective-permute-start | bytes 786440 | tf_op jit(solution)/shard_map/ppermute | solution.py:256
  7.7 0.8 copy.14
  8.5 1.3 %collective-permute-done.beyond = f32[4,128,128]{2,1,0:T(8,128)S(1)} collective-permute-done((f32[4,128,128]{2,1,0:T(8,128)S(1)}, f32[4,128,128]{2,1,0:T(8,128)S(1)}, u32[]{:S(2)}, u32[]{:S(2)}) %collective-permute-start) | collective-permute-done | bytes 262176 | tf_op jit(solution)/shard_map/ppermute | solution.py:255
  9.8 0.0 copy-start
  9.8 1.2 copy-done
  11.0 0.7 copy-done.12
  11.7 0.0 copy-start.14
  11.8 0.7 copy-done.14
  12.5 0.0 copy-start.16
  12.5 0.7 copy-done.16
  13.2 19.4 %shard_map.73 = (f32[128,4,128]{2,1,0:T(4,128)}, s32[1,4096]{1,0:T(1,128)S(1)}) custom-call(f32[4,4,128,128]{3,2,1,0:T(8,128)S(1)} %bitcast.17, f32[4,128,128]{2,1,0:T(8,128)S(1)} %collective-permute-done.beyond, s32[1,4096]{1,0:T(1,128)S(1)} %copy-done.12, f32[3,4096]{1,0:T(4,128)S(1)} %bitcast.24, s32[1,4096]{1,0:T(1,128)S(1)} %bitcast.26, ...), custom_call_target="tpu_custom_call" | custom-call | tf_op jit(solution)/shard_map/pallas_call | solution.py:113
  32.6 11.7 %all-to-all-start = ((f32[128,4,128]{2,1,0:T(4,128)}), f32[128,4,128]{2,1,0:T(4,128)S(1)}, u32[]{:S(2)}, u32[]{:S(2)}) async-start(f32[128,4,128]{2,1,0:T(4,128)} %get-tuple-element.11), calls=%async_computation | async-start | bytes 524288 | tf_op jit(solution)/shard_map/all_to_all | solution.py:261
  44.4 0.0 collective-permute-done.1.below
  44.4 0.0 copy-done.1
  44.4 0.0 copy-start.2
  44.4 1.7 %copy-done.2 = f32[1,9,4,128,128]{4,3,2,1,0:T(8,128)S(1)} copy-done((f32[1,9,4,128,128]{4,3,2,1,0:T(8,128)S(1)}, f32[1,9,4,128,128]{4,3,2,1,0:T(8,128)}, u32[]{:S(2)}) %copy-start.2) | copy-done | bytes 2359320
  46.1 0.0 copy-start.4
  46.1 0.9 copy-done.4
  47.0 1.0 shard_map.74.refs_2_
  48.0 0.0 copy-start.5
  48.0 7.1 %all-to-all-done.refs_0_ = f32[128,4,128]{2,1,0:T(4,128)S(1)} async-done(((f32[128,4,128]{2,1,0:T(4,128)}), f32[128,4,128]{2,1,0:T(4,128)S(1)}, u32[]{:S(2)}, u32[]{:S(2)}) %all-to-all-start) | async-done | bytes 262176 | tf_op jit(solution)/shard_map/all_to_all | solution.py:261
  55.2 0.0 copy-start.6
  55.2 0.7 copy-done.6
  55.9 0.0 copy-start.7
  55.9 0.9 copy-done.7
  56.8 13.2 %shard_map.75 = (s32[64,128]{1,0:T(8,128)S(1)}, f32[4,128,128]{2,1,0:T(8,128)S(1)}, f32[4,4,128,128]{3,2,1,0:T(8,128)S(1)}, f32[4,4,128,128]{3,2,1,0:T(8,128)S(1)}) custom-call(f32[128,4,128]{2,1,0:T(4,128)S(1)} %copy-done.7, f32[4,4,128,128]{3,2,1,0:T(8,128)S(1)} %bitcast.19, f32[4,4,128,128]{3,2,1,0:T(8,128)S(1)} %shard_map.74.refs_2_), custom_call_target="tpu_custom_call" | custom-call | tf_op jit(solution)/shard_map/pallas_call | solution.py:229
  70.0 0.0 copy-start.10
  70.0 0.7 copy-done.10
  70.8 2.9 %collective-permute-start.2 = (f32[4,128,128]{2,1,0:T(8,128)S(1)}, f32[4,128,128]{2,1,0:T(8,128)S(1)}, u32[]{:S(2)}, u32[]{:S(2)}) collective-permute-start(f32[4,128,128]{2,1,0:T(8,128)S(1)} %get-tuple-element.18), channel_id=1, source_target_pairs={{1,0},{2,1},{3,2},{4,3},{5,4},{6,5},{7,6},{8,7},{9,8},{10,9},{11,1... | collective-permute-start | bytes 786440 | tf_op jit(solution)/shard_map/ppermute | solution.py:255
  73.7 2.6 %collective-permute-start.3 = (f32[4,128,128]{2,1,0:T(8,128)S(1)}, f32[4,128,128]{2,1,0:T(8,128)S(1)}, u32[]{:S(2)}, u32[]{:S(2)}) collective-permute-start(f32[4,128,128]{2,1,0:T(8,128)S(1)} %get-tuple-element.17), channel_id=1, source_target_pairs={{0,1},{1,2},{2,3},{3,4},{4,5},{5,6},{6,7},{7,8},{8,9},{9,10},{10,1... | collective-permute-start | bytes 786440 | tf_op jit(solution)/shard_map/ppermute | solution.py:256
  76.4 2.1 %collective-permute-done.2.beyond = f32[4,128,128]{2,1,0:T(8,128)S(1)} collective-permute-done((f32[4,128,128]{2,1,0:T(8,128)S(1)}, f32[4,128,128]{2,1,0:T(8,128)S(1)}, u32[]{:S(2)}, u32[]{:S(2)}) %collective-permute-start.2) | collective-permute-done | bytes 262176 | tf_op jit(solution)/shard_map/ppermute | solution.py:255
  78.5 0.0 copy-done.8
  78.5 0.0 copy-done.13
  78.5 0.0 copy-done.15
  78.5 17.6 %shard_map.76 = f32[128,2,128]{2,1,0:T(2,128)} custom-call(f32[4,4,128,128]{3,2,1,0:T(8,128)S(1)} %get-tuple-element.12.state.refs_1_, f32[4,128,128]{2,1,0:T(8,128)S(1)} %collective-permute-done.2.beyond, s32[1,4096]{1,0:T(1,128)S(1)} %copy-done.13, f32[3,4096]{1,0:T(4,128)S(1)} %bitcast.25, s32[1,4096]{1,0:T(1,128)S(1)} %bitcast.27, ...), custom_call_target="tpu_custom_call" | custom-call | tf_op jit(solution)/shard_map/pallas_call | solution.py:119
  96.1 5.8 %all-to-all-start.1 = ((f32[128,2,128]{2,1,0:T(2,128)}), f32[128,2,128]{2,1,0:T(2,128)S(1)}, u32[]{:S(2)}, u32[]{:S(2)}) async-start(f32[128,2,128]{2,1,0:T(2,128)} %shard_map.76), calls=%async_computation.1 | async-start | bytes 262144 | tf_op jit(solution)/shard_map/all_to_all | solution.py:261
  101.9 0.0 collective-permute-done.3.below
  101.9 0.0 copy-done.5
  101.9 0.0 copy-start.3
  101.9 1.7 %copy-done.3 = f32[1,9,4,128,128]{4,3,2,1,0:T(8,128)S(1)} copy-done((f32[1,9,4,128,128]{4,3,2,1,0:T(8,128)S(1)}, f32[1,9,4,128,128]{4,3,2,1,0:T(8,128)}, u32[]{:S(2)}) %copy-start.3) | copy-done | bytes 2359320
  103.6 1.0 shard_map.77.refs_2_
  104.6 7.3 %all-to-all-done.1.refs_0_ = f32[128,2,128]{2,1,0:T(2,128)S(1)} async-done(((f32[128,2,128]{2,1,0:T(2,128)}), f32[128,2,128]{2,1,0:T(2,128)S(1)}, u32[]{:S(2)}, u32[]{:S(2)}) %all-to-all-start.1) | async-done | bytes 131104 | tf_op jit(solution)/shard_map/all_to_all | solution.py:261
  111.8 0.0 copy-done.11
  111.8 1.2 copy-done.9
  113.1 11.8 %shard_map.78 = f32[4,4,128,128]{3,2,1,0:T(8,128)} custom-call(f32[128,2,128]{2,1,0:T(2,128)S(1)} %all-to-all-done.1.refs_0_, f32[4,4,128,128]{3,2,1,0:T(8,128)S(1)} %get-tuple-element.12.state.refs_1_, f32[4,4,128,128]{3,2,1,0:T(8,128)S(1)} %shard_map.77.refs_2_, s32[64,128]{1,0:T(8,128)S(1)} %get-tuple-element.14.refs_3_, f32[4,128,128]{2,1,0:T(8,128)S(1)} %copy-done.11, ...), custom_call_target="tpu_custom_call" | custom-call | tf_op jit(solution)/shard_map/pallas_call | solution.py:243
  (7 shorter events, 0.0 us)
Async XLA Ops:
  0.0 44.4 %copy-start.1 = (f32[1,4,4,128,128]{4,3,2,1,0:T(8,128)S(1)}, f32[1,4,4,128,128]{4,3,2,1,0:T(8,128)}, u32[]{:S(2)}) copy-start(f32[1,4,4,128,128]{4,3,2,1,0:T(8,128)} %param.7) | copy-start | bytes 3145732
  1.2 8.6 %collective-permute-start = (f32[4,128,128]{2,1,0:T(8,128)S(1)}, f32[4,128,128]{2,1,0:T(8,128)S(1)}, u32[]{:S(2)}, u32[]{:S(2)}) collective-permute-start(f32[4,128,128]{2,1,0:T(8,128)S(1)} %get-tuple-element.20), channel_id=1, source_target_pairs={{1,0},{2,1},{3,2},{4,3},{5,4},{6,5},{7,6},{8,7},{9,8},{10,9},{11,1... | collective-permute-start | bytes 786440 | tf_op jit(solution)/shard_map/ppermute | solution.py:255
  4.5 39.9 %collective-permute-start.1 = (f32[4,128,128]{2,1,0:T(8,128)S(1)}, f32[4,128,128]{2,1,0:T(8,128)S(1)}, u32[]{:S(2)}, u32[]{:S(2)}) collective-permute-start(f32[4,128,128]{2,1,0:T(8,128)S(1)} %get-tuple-element.19), channel_id=1, source_target_pairs={{0,1},{1,2},{2,3},{3,4},{4,5},{5,6},{6,7},{7,8},{8,9},{9,10},{10,1... | collective-permute-start | bytes 786440 | tf_op jit(solution)/shard_map/ppermute | solution.py:256
  9.8 1.2 copy-start
  11.0 0.7 copy-start.12
  11.7 0.7 copy-start.14
  12.5 0.7 copy-start.16
  32.6 22.5 %all-to-all-start = ((f32[128,4,128]{2,1,0:T(4,128)}), f32[128,4,128]{2,1,0:T(4,128)S(1)}, u32[]{:S(2)}, u32[]{:S(2)}) async-start(f32[128,4,128]{2,1,0:T(4,128)} %get-tuple-element.11), calls=%async_computation | async-start | bytes 524288 | tf_op jit(solution)/shard_map/all_to_all | solution.py:261
  44.4 1.7 %copy-start.2 = (f32[1,9,4,128,128]{4,3,2,1,0:T(8,128)S(1)}, f32[1,9,4,128,128]{4,3,2,1,0:T(8,128)}, u32[]{:S(2)}) copy-start(f32[1,9,4,128,128]{4,3,2,1,0:T(8,128)} %param.8) | copy-start | bytes 7077892
  46.1 0.9 copy-start.4
  48.0 53.9 %copy-start.5 = (f32[1,4,128,128]{3,2,1,0:T(8,128)S(1)}, f32[1,4,128,128]{3,2,1,0:T(8,128)}, u32[]{:S(2)}) copy-start(f32[1,4,128,128]{3,2,1,0:T(8,128)} %param.9) | copy-start | bytes 786436
  55.2 0.7 copy-start.6
  55.9 0.9 copy-start.7
  56.8 21.7 %copy-start.13 = (s32[1,4096]{1,0:T(1,128)S(1)}, s32[1,4096]{1,0:T(1,128)}, u32[]{:S(2)}) copy-start(s32[1,4096]{1,0:T(1,128)} %donor.3) | copy-start | bytes 49156
  56.8 21.7 %copy-start.15 = (s32[1,4096,1]{1,2,0:T(1,128)S(1)}, s32[1,4096,1]{1,2,0:T(1,128)}, u32[]{:S(2)}) copy-start(s32[1,4096,1]{1,2,0:T(1,128)} %param.12) | copy-start | bytes 49156
  70.0 0.7 copy-start.10
  70.7 7.7 %copy-start.8 = (f32[4,4,128,128]{3,2,1,0:T(8,128)}, f32[4,4,128,128]{3,2,1,0:T(8,128)S(1)}, u32[]{:S(2)}) copy-start(f32[4,4,128,128]{3,2,1,0:T(8,128)S(1)} %get-tuple-element.16.refs_5_) | copy-start | bytes 3145732
  70.8 7.7 %collective-permute-start.2 = (f32[4,128,128]{2,1,0:T(8,128)S(1)}, f32[4,128,128]{2,1,0:T(8,128)S(1)}, u32[]{:S(2)}, u32[]{:S(2)}) collective-permute-start(f32[4,128,128]{2,1,0:T(8,128)S(1)} %get-tuple-element.18), channel_id=1, source_target_pairs={{1,0},{2,1},{3,2},{4,3},{5,4},{6,5},{7,6},{8,7},{9,8},{10,9},{11,1... | collective-permute-start | bytes 786440 | tf_op jit(solution)/shard_map/ppermute | solution.py:255
  73.7 28.1 %collective-permute-start.3 = (f32[4,128,128]{2,1,0:T(8,128)S(1)}, f32[4,128,128]{2,1,0:T(8,128)S(1)}, u32[]{:S(2)}, u32[]{:S(2)}) collective-permute-start(f32[4,128,128]{2,1,0:T(8,128)S(1)} %get-tuple-element.17), channel_id=1, source_target_pairs={{0,1},{1,2},{2,3},{3,4},{4,5},{5,6},{6,7},{7,8},{8,9},{9,10},{10,1... | collective-permute-start | bytes 786440 | tf_op jit(solution)/shard_map/ppermute | solution.py:256
  96.1 15.8 %all-to-all-start.1 = ((f32[128,2,128]{2,1,0:T(2,128)}), f32[128,2,128]{2,1,0:T(2,128)S(1)}, u32[]{:S(2)}, u32[]{:S(2)}) async-start(f32[128,2,128]{2,1,0:T(2,128)} %shard_map.76), calls=%async_computation.1 | async-start | bytes 262144 | tf_op jit(solution)/shard_map/all_to_all | solution.py:261
  101.9 1.7 %copy-start.3 = (f32[1,9,4,128,128]{4,3,2,1,0:T(8,128)S(1)}, f32[1,9,4,128,128]{4,3,2,1,0:T(8,128)}, u32[]{:S(2)}) copy-start(f32[1,9,4,128,128]{4,3,2,1,0:T(8,128)} %param.8) | copy-start | bytes 7077892
  103.6 8.3 %copy-start.11 = (f32[4,128,128]{2,1,0:T(8,128)S(1)}, f32[4,128,128]{2,1,0:T(8,128)}, u32[]{:S(2)}) copy-start(f32[4,128,128]{2,1,0:T(8,128)} %copy-done.10) | copy-start | bytes 786436
  111.8 1.2 copy-start.9

commit v2 on v1

v2 whole, which is shorter than its diff:
```python
import functools
import jax
import jax.numpy as jnp
from jax import lax
from jax.experimental import pallas as pl
from jax.experimental.pallas import tpu as pltpu
from jax.sharding import PartitionSpec as P

step_size = 0.4
f32, bf16, i32 = jnp.float32, jnp.bfloat16, jnp.int32
VMEM_LIMIT = 40 * 1024 * 1024
NT = (((1,), (1,)), ((), ()))


def iota(shape, dim):
    return lax.broadcasted_iota(i32, shape, dim)


def two_parts(x):
    high = x.astype(bf16)
    low = (x - high.astype(f32)).astype(bf16)
    return high, low


def params():
    return pltpu.CompilerParams(vmem_limit_bytes=VMEM_LIMIT)


TILE = 256
GROUP = 4
DONOR_ROWS = 24
ARRIVAL_ROWS = 40


def placed(kinds):
    spaces = {"v": pltpu.VMEM, "s": pltpu.SMEM, "h": pltpu.HBM}
    return [pl.BlockSpec(memory_space=spaces[kind]) for kind in kinds]


def exact(mask):
    return mask.astype(f32).astype(bf16)


def starts_of(counts):
    tiles = [(count + TILE - 1) // TILE for count in counts]
    first = tiles[0]
    second = first + tiles[1]
    third = second + tiles[2]
    return first, second, third, third + tiles[3]


def bucket_of(t, starts):
    return sum((t >= starts[i]).astype(i32) for i in range(3))


def prepare_kernel(donor, fractions, dest, recept, table, labels, starts, total):
    width = 512
    rows = donor.shape[1]
    plane_all = donor[...] >> 14
    counts = [jnp.sum((plane_all == p + 1).astype(f32)).astype(i32) for p in range(4)]
    begin = starts_of(counts)
    for i in range(4):
        starts[i] = begin[i]
    offsets = (0,) + begin[:3]
    total[...] = jnp.zeros_like(total)
    labels[...] = jnp.zeros_like(labels)
    blocks = iota((144, width), 0)
    slots = iota((64, width), 0)
    high_rows = iota((DONOR_ROWS, width), 0)
    low_rows = iota((TILE, width), 0)
    before = exact(iota((width, width), 0) < iota((width, width), 1))
    blank = jnp.zeros((8, width), f32)

    def step(t, counted):
        here = pl.ds(pl.multiple_of(t * width, width), width)
        base = donor[:, here]
        plane = base >> 14
        target = dest[:, here]
        member = ((blocks == target) | (blocks == plane + 127)).astype(f32)
        member_b = member.astype(bf16)
        earlier = jnp.dot(member_b, before, preferred_element_type=f32) + counted
        ranked = member * earlier
        rank = jnp.sum(ranked[:128], axis=0, keepdims=True)
        spot = jnp.sum(ranked[128:], axis=0, keepdims=True).astype(i32)
        counted = counted + jnp.sum(member, axis=1, keepdims=True)
        offset = jnp.where(plane == 1, offsets[0], jnp.where(plane == 2, offsets[1], jnp.where(plane == 3, offsets[2], offsets[3])))
        high = offset + (spot >> 8)
        low = spot & 255
        chosen = high_rows == high
        fields = [((base >> 7) & 127).astype(f32), (base & 127).astype(f32), target.astype(f32), rank + 1.0]
        for i in range(3):
            rest = fractions[i, :, here]
            for _ in range(3):
                part = rest.astype(bf16).astype(f32)
                fields.append(part)
                rest = rest - part
        spread = jnp.concatenate([jnp.where(chosen, field, 0.0) for field in fields] + [blank], axis=0)
        total[...] += lax.dot_general(spread.astype(bf16), exact(low_rows == low), NT, preferred_element_type=f32)
        held = slots == rank.astype(i32)
        label = recept[:, here] + 1
        marks = [jnp.where(held, part.astype(f32), 0.0) for part in (label >> 8, label & 255)]
        marks = jnp.concatenate(marks, axis=0).astype(bf16)
        labels[...] += lax.dot_general(member_b[:128], marks, NT, preferred_element_type=f32)
        return counted

    lax.fori_loop(0, rows // width, step, jnp.zeros((144, 1), f32))

    def field(i):
        return total[i * DONOR_ROWS : (i + 1) * DONOR_ROWS]

    for i in range(4):
        table[i] = field(i)
    for i in range(3):
        table[4 + i] = field(4 + 3 * i) + field(5 + 3 * i) + field(6 + 3 * i)
    both = labels[...] * jnp.where(iota((128, 128), 1) < 64, 256.0, 1.0)
    labels[...] = both + pltpu.roll(both, 64, 1)


def prepare(donor, fractions, dest, recept):
    return pl.pallas_call(
        prepare_kernel,
        out_shape=(
            jax.ShapeDtypeStruct((7, DONOR_ROWS, TILE), f32),
            jax.ShapeDtypeStruct((128, 128), f32),
            jax.ShapeDtypeStruct((4,), i32),
        ),
        in_specs=placed("vvvv"),
        out_specs=tuple(placed("vvs")),
        scratch_shapes=[pltpu.VMEM((13 * DONOR_ROWS + 8, TILE), f32)],
        compiler_params=params(),
        cost_estimate=pl.CostEstimate(flops=3 * 10**9, bytes_accessed=10**6, transcendentals=0),
    )(donor, fractions, dest, recept)


def pack_kernel(with_labels, fetched, below, beyond, table, starts, *rest):
    del below
    if with_labels:
        labels, out, source, total, state, sems = rest
    else:
        out, source, total, state, sems = rest
    copies = [pltpu.make_async_copy(fetched.at[c], state.at[c], sems.at[c]) for c in range(4)]
    for copy in copies:
        copy.start()
    for c in range(4):
        copies[c].wait()
        rows = slice(c * 128, c * 128 + 128)
        for x in range(5):
            high, low = two_parts(state[c, x] if x < 4 else beyond[c])
            for pair, side in ((x, 0), (x - 1, 128)):
                if 0 <= pair < 4:
                    for begin, part in ((0, high), (256, low), (512, high)):
                        source[pair, rows, begin + side : begin + side + 128] = part
    total[...] = jnp.zeros_like(total)
    cells = iota((128, TILE), 0)
    slots = iota((64, TILE), 0)
    begin = tuple(starts[i] for i in range(4))

    def interpolated(t):
        line, point, target, rank, fx, fy, fz = (table[i, pl.ds(t, 1), :] for i in range(7))
        line, point, target, rank = (v.astype(i32) for v in (line, point, target, rank))
        wy = jnp.where(cells == line, 1.0 - fy, jnp.where(cells == line + 1, fy, 0.0))
        wz = jnp.where(cells == point, 1.0 - fz, jnp.where(cells == point + 1, fz, 0.0))
        first, second = two_parts(wz * (1.0 - fx)), two_parts(wz * fx)
        high = [first[0], second[0]]
        weights = jnp.concatenate(high + high + [first[1], second[1]], axis=0)
        lines = jnp.dot(source[bucket_of(t, begin)], weights, preferred_element_type=f32)
        chosen = slots == rank - 1
        values = [jnp.sum(lines[c * 128 : c * 128 + 128] * wy, axis=0, keepdims=True) for c in range(4)]
        parts = []
        for which in (0, 1):
            for c in range(4):
                part = two_parts(values[c])[which].astype(f32)
                parts.append(jnp.where(chosen, part, 0.0).astype(bf16))
        return exact(cells == target), jnp.concatenate(parts, axis=0)

    def step(t, _):
        members, packed = zip(*[interpolated(t * GROUP + j) for j in range(GROUP)])
        members, packed = jnp.concatenate(members, axis=1), jnp.concatenate(packed, axis=1)
        total[...] += lax.dot_general(members, packed, NT, preferred_element_type=f32)
        return 0

    lax.fori_loop(0, (begin[3] + GROUP - 1) // GROUP, step, 0)
    for half in range(2):
        cut = slice(half * 128, half * 128 + 128)
        low = slice(256 + half * 128, 256 + half * 128 + 128)
        out[:, half, :] = total[:, cut] + total[:, low]
    if with_labels:
        out[:, 2, :] = labels[...]
        out[:, 3, :] = jnp.zeros((128, 128), f32)


def pack(state, below, beyond, table, starts, labels=None):
    first = labels is not None
    operands = (state, below, beyond, table, starts) + ((labels,) if first else ())
    return pl.pallas_call(
        functools.partial(pack_kernel, first),
        out_shape=jax.ShapeDtypeStruct((128, 4 if first else 2, 128), f32),
        in_specs=placed("hhvvsv"[: len(operands)]),
        out_specs=placed("v")[0],
        scratch_shapes=[
            pltpu.VMEM((4, 512, 768), bf16),
            pltpu.VMEM((128, 512), f32),
            pltpu.VMEM(state.shape, f32),
            pltpu.SemaphoreType.DMA((4,)),
        ],
        compiler_params=params(),
    )(*operands)


def rates_of(x, state, below, beyond, metric, damping):
    row = iota((128, 128), 0)
    lane = iota((128, 128), 1)

    def differences(c):
        here = state[c, x]
        low = below[c] if x == 0 else state[c, x - 1]
        high = beyond[c] if x == 3 else state[c, x + 1]
        up = jnp.where(row < 127, pltpu.roll(here, 127, 0), 0.0)
        down = jnp.where(row > 0, pltpu.roll(here, 1, 0), 0.0)
        right = jnp.where(lane < 127, pltpu.roll(here, 127, 1), 0.0)
        left = jnp.where(lane > 0, pltpu.roll(here, 1, 1), 0.0)
        return (high - low) * 0.5, (up - down) * 0.5, (right - left) * 0.5

    def gradient(diffs, i):
        return metric[i, x] * diffs[0] + metric[3 + i, x] * diffs[1] + metric[6 + i, x] * diffs[2]

    damp = damping[x]
    pressure = -damp * state[0, x]
    for i in range(3):
        pressure = pressure - gradient(differences(1 + i), i)
    diffs = differences(0)
    return [pressure] + [-gradient(diffs, i) - damp * state[1 + i, x] for i in range(3)]


def deposit_kernel(first, *refs):
    arrived, refs = refs[0], refs[1:]
    fetched, refs = refs[:5], refs[5:]
    if first:
        low_plane, high_plane, section, counts, base, spots, cells, starts, *scratch = refs
    else:
        counts, base, spots, cells, starts, out, *scratch = refs
    slots, sorted_, total, count, now, below, beyond, metric, damping, sems = scratch
    held = (now, below, beyond, metric, damping)
    copies = [pltpu.make_async_copy(fetched[i], held[i], sems.at[i]) for i in range(5)]
    for copy in copies:
        copy.start()
    lane = iota((64, 128), 1)

    def halves(j):
        first, second = arrived[0:64, j, :], arrived[64:128, j, :]
        return (
            jnp.where(lane < 64, first, pltpu.roll(second, 64, 1)),
            jnp.where(lane < 64, pltpu.roll(first, 64, 1), second),
        )

    values = halves(0) + halves(1)
    for c in range(4):
        high, low = two_parts(values[c])
        slots[c] = high.astype(f32)
        slots[4 + c] = low.astype(f32)
    fields = 8
    if first:
        fields = 10
        label = halves(2)[0].astype(i32) - 1
        pair = jnp.where(label >= 0, label >> 15, -1)
        slots[8] = ((label >> 7) & 127).astype(f32)
        slots[9] = ((label & 127) + ((label >> 14) & 1) * 128 + 1).astype(f32)
        member = [(pair == p).astype(f32) for p in range(2)]
        sizes = [jnp.sum(m).astype(i32) for m in member]
        starts[0] = (sizes[0] + 2 * TILE - 1) // (2 * TILE)
        starts[1] = starts[0] + (sizes[1] + 2 * TILE - 1) // (2 * TILE)
        stacked = jnp.concatenate(member, axis=0).astype(bf16)
        before = exact(iota((128, 128), 0) < iota((128, 128), 1))
        inner = jnp.dot(stacked, before, preferred_element_type=f32)
        sums = [jnp.broadcast_to(jnp.sum(m, axis=1, keepdims=True), (64, 128)) for m in member]
        above = exact(iota((64, 64), 1) < iota((64, 64), 0))
        outer = jnp.dot(above, jnp.concatenate(sums, axis=1).astype(bf16), preferred_element_type=f32)
        spot = jnp.full((64, 128), -1, i32)
        for p in range(2):
            rank = (inner[p * 64 : p * 64 + 64] + outer[:, p * 128 : p * 128 + 128]).astype(i32)
            spot = jnp.where(pair == p, (starts[0] * (2 * TILE) if p else 0) + rank, spot)
        spots[...] = spot
    split, tiles = starts[0], starts[1]
    sorted_[...] = jnp.zeros_like(sorted_)
    total[...] = jnp.zeros_like(total)
    if first:
        count[...] = jnp.zeros_like(count)
    high_rows = iota((ARRIVAL_ROWS, 128), 0)
    low_rows = iota((TILE, 128), 0)
    chunk = 16

    def sort(t, _):
        spreads, places = [], []
        for j in range(chunk):
            row = pl.ds(t * chunk + j, 1)
            spot = spots[row, :]
            chosen = high_rows == (spot >> 8)
            spread = [jnp.where(chosen, slots[f, row, :], 0.0) for f in range(fields)]
            spreads.append(jnp.concatenate(spread, axis=0).astype(bf16))
            places.append(exact(low_rows == (spot & 255)))
        sorted_[...] += lax.dot_general(
            jnp.concatenate(spreads, axis=1), jnp.concatenate(places, axis=1), NT, preferred_element_type=f32
        )
        return 0

    lax.fori_loop(0, 64 // chunk, sort, 0)
    if first:
        cells[0] = sorted_[8 * ARRIVAL_ROWS : 9 * ARRIVAL_ROWS].astype(i32)
        cells[1] = sorted_[9 * ARRIVAL_ROWS : 10 * ARRIVAL_ROWS].astype(i32) - 1
    lines = iota((128, TILE), 0)
    points = iota((256, TILE), 0)

    def add(t, _):
        rows = [pl.ds(2 * t + h, 1) for h in range(2)]
        at = [lines == cells[0, row, :] for row in rows]
        selector = [exact(points == cells[1, row, :]) for row in rows]

        def spread(f):
            picked = [sorted_[pl.ds(f * ARRIVAL_ROWS + 2 * t + h, 1), :] for h in range(2)]
            return jnp.concatenate([jnp.where(at[h], picked[h], 0.0).astype(bf16) for h in range(2)], axis=1)

        high = jnp.concatenate([spread(f) for f in range(4)], axis=0)
        low = jnp.concatenate([spread(4 + f) for f in range(4)], axis=0)
        selector = jnp.concatenate(selector, axis=1)
        which = (t >= split).astype(i32)
        total[which] += lax.dot_general(
            jnp.concatenate([high, low], axis=1), jnp.concatenate([selector, selector], axis=1), NT, preferred_element_type=f32
        )
        if first:
            ones = jnp.concatenate([exact(a) for a in at], axis=1)
            count[which] += lax.dot_general(ones, selector, NT, preferred_element_type=f32)
        return 0

    lax.fori_loop(0, tiles, add, 0)
    for copy in copies:
        copy.wait()
    for x in range(4):
        lanes = slice((x % 2) * 128, (x % 2) * 128 + 128)
        if first:
            counts[x] = count[x // 2, :, lanes]
        rates = rates_of(x, now, below, beyond, metric, damping)
        for c in range(4):
            fringe = total[x // 2, c * 128 : c * 128 + 128, lanes]
            rate = rates[c] + fringe - counts[x] * now[c, x]
            if first:
                section[c, x] = now[c, x] + step_size * rate
                if x in (0, 3):
                    (low_plane if x == 0 else high_plane)[c] = section[c, x]
                base[c, x] = now[c, x] + (0.5 * step_size) * rate
            else:
                out[c, x] = base[c, x] + (0.5 * step_size) * rate


def deposit(first, arrived, *operands):
    fields = 10 if first else 8
    fetched = operands[:5]
    shape = fetched[0].shape
    if first:
        results = (
            jax.ShapeDtypeStruct((4, 128, 128), f32),
            jax.ShapeDtypeStruct((4, 128, 128), f32),
            jax.ShapeDtypeStruct(shape, f32),
            jax.ShapeDtypeStruct(shape[1:], f32),
            jax.ShapeDtypeStruct(shape, f32),
            jax.ShapeDtypeStruct((64, 128), i32),
            jax.ShapeDtypeStruct((2, ARRIVAL_ROWS, TILE), i32),
            jax.ShapeDtypeStruct((2,), i32),
        )
        specs, result_specs = placed("vhhhhh"), tuple(placed("vvvvvvvs"))
    else:
        results, result_specs = jax.ShapeDtypeStruct(shape, f32), placed("v")[0]
        specs = placed("vhhhhhvvvvs")
    return pl.pallas_call(
        functools.partial(deposit_kernel, first),
        out_shape=results,
        in_specs=specs,
        out_specs=result_specs,
        scratch_shapes=[
            pltpu.VMEM((fields, 64, 128), f32),
            pltpu.VMEM((fields * ARRIVAL_ROWS, TILE), f32),
            pltpu.VMEM((2, 512, 256), f32),
            pltpu.VMEM((2, 128, 256), f32),
        ]
        + [pltpu.VMEM(operand.shape, f32) for operand in fetched]
        + [pltpu.SemaphoreType.DMA((5,))],
        compiler_params=params(),
    )(arrived, *operands)


def neighbours(low_plane, high_plane):
    count = lax.axis_size("blk")
    forward = [(i, i + 1) for i in range(count - 1)]
    backward = [(i + 1, i) for i in range(count - 1)]
    beyond = lax.ppermute(low_plane, "blk", backward)
    below = lax.ppermute(high_plane, "blk", forward)
    return below, beyond


def exchange(outgoing):
    return lax.all_to_all(outgoing, ("grid", "blk"), split_axis=0, concat_axis=0, tiled=True)


def local(state, metric, damping, donor, fractions, dest, recept):
    state, metric, damping = state[0], metric[0], damping[0]
    fractions = fractions.reshape(3, 1, -1)
    dest = dest.reshape(1, -1)
    below, beyond = neighbours(state[:, 0], state[:, 3])
    table, labels, tiles = prepare(donor, fractions, dest, recept)
    arrived = exchange(pack(state, below, beyond, table, tiles, labels))
    low_plane, high_plane, section, *kept = deposit(True, arrived, state, below, beyond, metric, damping)
    below, beyond = neighbours(low_plane, high_plane)
    arrived = exchange(pack(section, below, beyond, table, tiles))
    return deposit(False, arrived, section, below, beyond, metric, damping, *kept)[None]


def solution(mesh):
    in_specs = (
        P("grid", None, "blk", None, None),
        P("grid", None, "blk", None, None),
        P("grid", "blk", None, None),
        P("grid", "blk"),
        P("grid", None, "blk"),
        P("grid", "blk", None),
        P("grid", "blk"),
    )
    out_specs = P("grid", None, "blk", None, None)
    return jax.shard_map(local, mesh=mesh, in_specs=in_specs, out_specs=out_specs, check_vma=False)
```

time: 126 us -> 105 us (0.83)
  the two profiles are of different devices: /device:TPU:1 before, /device:TPU:0 now
where the time goes in v2:
time: 105 us
  Pallas kernels  47.4 us (45%)
  blocking collectives  46.5 us (44%)
  starting transfers between devices  6.94 us (7%)
  waiting for transfers between devices  2.13 us (2%)
  local copies, waits for them, and re-layouts  1.41 us (1%)
    all_to_all x2, blocking collectives, exchange(): lax.all_to_all(outgoing, ('grid', 'blk'), split_axis=0, concat_axis=0, ti...  46.5 us
    pallas_call x2, Pallas kernels, deposit(): pl.pallas_call(functools.partial(deposit_kernel, first), out_shape=result...  26.1 us
    pallas_call x2, Pallas kernels, pack(): pl.pallas_call(functools.partial(pack_kernel, first), out_shape=jax.Shape...  15.8 us
    pallas_call x1, Pallas kernels, prepare(): pl.pallas_call(prepare_kernel, out_shape=(jax.ShapeDtypeStruct((7, DONOR_...  5.47 us
    ppermute x2, starting transfers between devices, neighbours(): below = lax.ppermute(high_plane, 'blk', forward)  4.35 us
    ppermute x2, starting transfers between devices, neighbours(): beyond = lax.ppermute(low_plane, 'blk', backward)  2.58 us
    ppermute x2, waiting for transfers between devices, neighbours(): beyond = lax.ppermute(low_plane, 'blk', backward)  2.12 us
  transfers between devices with their start and end apart: 4, of which 1 were waited for; matrix products, arithmetic and copies ran while one was open for 0% of the time, Pallas kernels for 5%

profile of v2, /device:TPU:0, one launch (start us, length us, event | category | flops | bytes accessed | tf_op | source)
XLA Modules:
  0.0 104.5 jit_solution(12276141782210265028)
XLA Ops:
  0.0 0.0 copy-start.6
  0.0 0.0 copy-start.5
  0.0 0.0 copy-start.3
  0.0 0.0 copy-start.4
  0.0 1.3 %copy.13 = f32[1,4,4,128,128]{4,3,1,2,0:T(8,128)S(1)} copy(f32[1,4,4,128,128]{4,3,2,1,0:T(8,128)} %param.7) | data formatting | bytes 2097152 | tf_op args[0]
  1.4 1.3 %collective-permute-start.1 = (f32[4,128,128]{2,1,0:T(8,128)S(1)}, f32[4,128,128]{2,1,0:T(8,128)S(1)}, u32[]{:S(2)}, u32[]{:S(2)}) collective-permute-start(f32[4,128,128]{2,1,0:T(8,128)S(1)} %get-tuple-element.27), channel_id=1, source_target_pairs={{1,0},{2,1},{3,2},{4,3},{5,4},{6,5},{7,6},{8,7},{9,8},{10,9},{11,1... | collective-permute-start | bytes 786440 | tf_op jit(solution)/shard_map/ppermute | solution.py:394
  2.7 3.0 %collective-permute-start = (f32[4,128,128]{2,1,0:T(8,128)S(1)}, f32[4,128,128]{2,1,0:T(8,128)S(1)}, u32[]{:S(2)}, u32[]{:S(2)}) collective-permute-start(f32[4,128,128]{2,1,0:T(8,128)S(1)} %get-tuple-element.28), channel_id=1, source_target_pairs={{0,1},{1,2},{2,3},{3,4},{4,5},{5,6},{6,7},{7,8},{8,9},{9,10},{10,1... | collective-permute-start | bytes 786440 | tf_op jit(solution)/shard_map/ppermute | solution.py:395
  5.8 0.0 copy-done.6
  5.8 0.0 copy-done.5
  5.8 0.0 copy-done.3
  5.8 0.0 copy-done.4
  5.8 0.0 copy-start
  5.8 0.0 copy-start.2
  5.8 5.5 %shard_map.73 = (f32[7,24,256]{2,1,0:T(8,128)S(1)}, f32[128,128]{1,0:T(8,128)S(1)}, s32[4]{0:T(128)S(1)}) custom-call(s32[1,4096]{1,0:T(1,128)S(1)} %copy-done.4, f32[3,1,4096]{2,1,0:T(1,128)S(1)} %bitcast.19, s32[1,4096]{1,0:T(1,128)S(1)} %bitcast.20, s32[1,4096]{1,0:T(1,128)S(1)} %copy-done.6), custom_call_target="tpu_custom_call" | custom-call | flops 3000000000 | bytes 1000000 | tf_op jit(solution)/shard_map/pallas_call | solution.py:120
  11.3 0.0 copy-start.1
  11.3 0.0 collective-permute-done.1.beyond.refs_3_
  11.3 0.0 collective-permute-done.below.refs_2_
  11.3 0.0 copy-done
  11.3 7.9 %shard_map.74 = f32[128,4,128]{2,1,0:T(4,128)S(1)} custom-call(f32[4,4,128,128]{3,2,1,0:T(8,128)S(1)} %bitcast.13, f32[4,128,128]{2,1,0:T(8,128)S(1)} %collective-permute-done.below.refs_2_, f32[4,128,128]{2,1,0:T(8,128)S(1)} %collective-permute-done.1.beyond.refs_3_, f32[7,24,256]{2,1,0:T(8,128)S(1)} %get-tuple-element.16.table, ...), custom_call_target="tpu_custom_call" | custom-call | tf_op jit(solution)/shard_map/pallas_call | solution.py:195
  19.3 24.2 %all_to_all.10.refs_0_ = f32[128,4,128]{2,1,0:T(4,128)S(1)} all-to-all(f32[128,4,128]{2,1,0:T(4,128)S(1)} %shard_map.74), channel_id=1, replica_groups=mesh['grid'=4,'blk'=32] {'grid','blk'}, dimensions={0} | all-to-all | bytes 524288 | tf_op jit(solution)/shard_map/all_to_all | solution.py:400
  43.5 0.0 copy-done.2
  43.5 0.0 copy-done.1
  43.5 13.0 %shard_map.75 = (f32[4,128,128]{2,1,0:T(8,128)S(1)}, f32[4,128,128]{2,1,0:T(8,128)S(1)}, f32[4,4,128,128]{3,2,1,0:T(8,128)S(1)}, f32[4,128,128]{2,1,0:T(8,128)S(...) custom-call(f32[128,4,128]{2,1,0:T(4,128)S(1)} %all_to_all.10.refs_0_, ...), custom_call_target="tpu_custom_call" | custom-call | tf_op jit(solution)/shard_map/pallas_call | solution.py:373
  56.5 1.3 %collective-permute-start.2 = (f32[4,128,128]{2,1,0:T(8,128)S(1)}, f32[4,128,128]{2,1,0:T(8,128)S(1)}, u32[]{:S(2)}, u32[]{:S(2)}) collective-permute-start(f32[4,128,128]{2,1,0:T(8,128)S(1)} %get-tuple-element.20), channel_id=1, source_target_pairs={{0,1},{1,2},{2,3},{3,4},{4,5},{5,6},{6,7},{7,8},{8,9},{9,10},{10,1... | collective-permute-start | bytes 786440 | tf_op jit(solution)/shard_map/ppermute | solution.py:395
  57.8 1.3 %collective-permute-start.3 = (f32[4,128,128]{2,1,0:T(8,128)S(1)}, f32[4,128,128]{2,1,0:T(8,128)S(1)}, u32[]{:S(2)}, u32[]{:S(2)}) collective-permute-start(f32[4,128,128]{2,1,0:T(8,128)S(1)} %get-tuple-element.21), channel_id=1, source_target_pairs={{1,0},{2,1},{3,2},{4,3},{5,4},{6,5},{7,6},{8,7},{9,8},{10,9},{11,1... | collective-permute-start | bytes 786440 | tf_op jit(solution)/shard_map/ppermute | solution.py:394
  59.1 0.0 collective-permute-done.2.below.refs_2_
  59.1 2.1 %collective-permute-done.3.beyond.refs_3_ = f32[4,128,128]{2,1,0:T(8,128)S(1)} collective-permute-done((f32[4,128,128]{2,1,0:T(8,128)S(1)}, f32[4,128,128]{2,1,0:T(8,128)S(1)}, u32[]{:S(2)}, u32[]{:S(2)}) %collective-permute-start.3) | collective-permute-done | bytes 262176 | tf_op jit(solution)/shard_map/ppermute | solution.py:394
  61.2 7.9 %shard_map.76 = f32[128,2,128]{2,1,0:T(2,128)S(1)} custom-call(f32[4,4,128,128]{3,2,1,0:T(8,128)S(1)} %get-tuple-element.19.fetched.refs_1_, f32[4,128,128]{2,1,0:T(8,128)S(1)} %collective-permute-done.2.below.refs_2_, f32[4,128,128]{2,1,0:T(8,128)S(1)} %collective-permute-done.3.beyond.refs_3_, f32[7,24,256]{2,1,0:T(8,128)S(1)} %get-tuple-element.16.table, ...), custom_call_target="tpu_custom_call" | custom-call | tf_op jit(solution)/shard_map/pallas_call | solution.py:195
  69.1 22.4 %all_to_all.11.refs_0_ = f32[128,2,128]{2,1,0:T(2,128)S(1)} all-to-all(f32[128,2,128]{2,1,0:T(2,128)S(1)} %shard_map.76), channel_id=1, replica_groups=mesh['grid'=4,'blk'=32] {'grid','blk'}, dimensions={0} | all-to-all | bytes 262144 | tf_op jit(solution)/shard_map/all_to_all | solution.py:400
  91.5 13.1 %shard_map.77 = f32[4,4,128,128]{3,2,1,0:T(8,128)} custom-call(f32[128,2,128]{2,1,0:T(2,128)S(1)} %all_to_all.11.refs_0_, f32[4,4,128,128]{3,2,1,0:T(8,128)S(1)} %get-tuple-element.19.fetched.refs_1_, f32[4,128,128]{2,1,0:T(8,128)S(1)} %collective-permute-done.2.below.refs_2_, f32[4,128,128]{2,1,0:T(8,128)S(1)} %collective-permute-done.3.beyond.refs_3_, ...), custom_call_target="tpu_custom_call" | custom-call | tf_op jit(solution)/shard_map/pallas_call | solution.py:373
  (1 shorter events, 0.0 us)
Async XLA Ops:
  0.0 5.8 %copy-start.6 = (s32[1,4096]{1,0:T(1,128)S(1)}, s32[1,4096]{1,0:T(1,128)}, u32[]{:S(2)}) copy-start(s32[1,4096]{1,0:T(1,128)} %recept.1) | copy-start | bytes 49156
  0.0 5.8 %copy-start.5 = (s32[1,4096,1]{1,2,0:T(1,128)S(1)}, s32[1,4096,1]{1,2,0:T(1,128)}, u32[]{:S(2)}) copy-start(s32[1,4096,1]{1,2,0:T(1,128)} %param.12) | copy-start | bytes 49156
  0.0 5.8 %copy-start.3 = (f32[1,3,4096]{2,0,1:T(1,128)S(1)}, f32[1,3,4096]{2,0,1:T(1,128)}, u32[]{:S(2)}) copy-start(f32[1,3,4096]{2,0,1:T(1,128)} %param.11) | copy-start | bytes 147460
  0.0 5.8 %copy-start.4 = (s32[1,4096]{1,0:T(1,128)S(1)}, s32[1,4096]{1,0:T(1,128)}, u32[]{:S(2)}) copy-start(s32[1,4096]{1,0:T(1,128)} %donor.1) | copy-start | bytes 49156
  1.4 9.9 %collective-permute-start.1 = (f32[4,128,128]{2,1,0:T(8,128)S(1)}, f32[4,128,128]{2,1,0:T(8,128)S(1)}, u32[]{:S(2)}, u32[]{:S(2)}) collective-permute-start(f32[4,128,128]{2,1,0:T(8,128)S(1)} %get-tuple-element.27), channel_id=1, source_target_pairs={{1,0},{2,1},{3,2},{4,3},{5,4},{6,5},{7,6},{8,7},{9,8},{10,9},{11,1... | collective-permute-start | bytes 786440 | tf_op jit(solution)/shard_map/ppermute | solution.py:394
  2.7 8.6 %collective-permute-start = (f32[4,128,128]{2,1,0:T(8,128)S(1)}, f32[4,128,128]{2,1,0:T(8,128)S(1)}, u32[]{:S(2)}, u32[]{:S(2)}) collective-permute-start(f32[4,128,128]{2,1,0:T(8,128)S(1)} %get-tuple-element.28), channel_id=1, source_target_pairs={{0,1},{1,2},{2,3},{3,4},{4,5},{5,6},{6,7},{7,8},{8,9},{9,10},{10,1... | collective-permute-start | bytes 786440 | tf_op jit(solution)/shard_map/ppermute | solution.py:395
  5.8 5.5 %copy-start = (f32[1,4,4,128,128]{4,3,2,1,0:T(8,128)S(1)}, f32[1,4,4,128,128]{4,3,2,1,0:T(8,128)}, u32[]{:S(2)}) copy-start(f32[1,4,4,128,128]{4,3,2,1,0:T(8,128)} %param.7) | copy-start | bytes 3145732
  5.8 37.6 %copy-start.2 = (f32[1,4,128,128]{3,2,1,0:T(8,128)S(1)}, f32[1,4,128,128]{3,2,1,0:T(8,128)}, u32[]{:S(2)}) copy-start(f32[1,4,128,128]{3,2,1,0:T(8,128)} %param.9) | copy-start | bytes 786436
  11.3 32.2 %copy-start.1 = (f32[1,9,4,128,128]{4,3,2,1,0:T(8,128)S(1)}, f32[1,9,4,128,128]{4,3,2,1,0:T(8,128)}, u32[]{:S(2)}) copy-start(f32[1,9,4,128,128]{4,3,2,1,0:T(8,128)} %param.8) | copy-start | bytes 7077892
  56.5 2.6 %collective-permute-start.2 = (f32[4,128,128]{2,1,0:T(8,128)S(1)}, f32[4,128,128]{2,1,0:T(8,128)S(1)}, u32[]{:S(2)}, u32[]{:S(2)}) collective-permute-start(f32[4,128,128]{2,1,0:T(8,128)S(1)} %get-tuple-element.20), channel_id=1, source_target_pairs={{0,1},{1,2},{2,3},{3,4},{4,5},{5,6},{6,7},{7,8},{8,9},{9,10},{10,1... | collective-permute-start | bytes 786440 | tf_op jit(solution)/shard_map/ppermute | solution.py:395
  57.8 3.4 %collective-permute-start.3 = (f32[4,128,128]{2,1,0:T(8,128)S(1)}, f32[4,128,128]{2,1,0:T(8,128)S(1)}, u32[]{:S(2)}, u32[]{:S(2)}) collective-permute-start(f32[4,128,128]{2,1,0:T(8,128)S(1)} %get-tuple-element.21), channel_id=1, source_target_pairs={{1,0},{2,1},{3,2},{4,3},{5,4},{6,5},{7,6},{8,7},{9,8},{10,9},{11,1... | collective-permute-start | bytes 786440 | tf_op jit(solution)/shard_map/ppermute | solution.py:394

commit v3 on v2

v3 whole, which is shorter than its diff:
```python
import functools
import jax
import jax.numpy as jnp
from jax import lax
from jax.experimental import pallas as pl
from jax.experimental.pallas import tpu as pltpu
from jax.sharding import PartitionSpec as P

step_size = 0.4
f32, bf16, i32 = jnp.float32, jnp.bfloat16, jnp.int32
VMEM_LIMIT = 40 * 1024 * 1024
NT = (((1,), (1,)), ((), ()))


def iota(shape, dim):
    return lax.broadcasted_iota(i32, shape, dim)


def two_parts(x):
    high = x.astype(bf16)
    low = (x - high.astype(f32)).astype(bf16)
    return high, low


def params():
    return pltpu.CompilerParams(vmem_limit_bytes=VMEM_LIMIT)


TILE = 256
GROUP = 10
DONOR_ROWS = 24
RANKS = 16


def placed(kinds):
    spaces = {"v": pltpu.VMEM, "s": pltpu.SMEM, "h": pltpu.HBM}
    return [pl.BlockSpec(memory_space=spaces[kind]) for kind in kinds]


def exact(mask):
    return mask.astype(f32).astype(bf16)


def starts_of(counts):
    tiles = [(count + TILE - 1) // TILE for count in counts]
    first = tiles[0]
    second = first + tiles[1]
    third = second + tiles[2]
    return first, second, third, third + tiles[3]


def bucket_of(t, starts):
    return sum((t >= starts[i]).astype(i32) for i in range(3))


def prepare_kernel(donor, fractions, dest, recept, table, labels, starts):
    chunks = [slice(i, i + TILE) for i in range(0, donor.shape[1], TILE)]
    plane_all = donor[...] >> 14
    counts = [jnp.sum((plane_all == p + 1).astype(f32)).astype(i32) for p in range(4)]
    begin = starts_of(counts)
    for i in range(4):
        starts[i] = begin[i]
    offsets = (0,) + begin[:3]
    blocks = iota((144, TILE), 0)
    slots = iota((64, TILE), 0)
    high_rows = iota((DONOR_ROWS, TILE), 0)
    low_rows = iota((TILE, TILE), 0)
    before = exact(iota((TILE, TILE), 0) < iota((TILE, TILE), 1))
    blank = jnp.zeros((8, TILE), f32)

    members = []
    for here in chunks:
        member = (blocks == dest[:, here]) | (blocks == (donor[:, here] >> 14) + 127)
        amount = jnp.where((blocks < 128) & (recept[:, here] >= 32768), 128.0, 1.0)
        members.append(jnp.where(member, amount, 0.0))
    earlier = jnp.dot(jnp.concatenate(members, axis=0).astype(bf16), before, preferred_element_type=f32)
    counted = jnp.zeros((144, 1), f32)
    spreads, places, targets, marks = [], [], [], []
    for i, here in enumerate(chunks):
        inside = members[i] > 0.0
        ranked = jnp.where(inside, earlier[i * 144 : i * 144 + 144] + counted, 0.0)
        counted = counted + jnp.sum(members[i], axis=1, keepdims=True)
        rank = jnp.sum(ranked[:128], axis=0, keepdims=True).astype(i32)
        spot = jnp.sum(ranked[128:], axis=0, keepdims=True).astype(i32)
        label = recept[:, here]
        rank = jnp.where(label >= 32768, 63 - (rank >> 7), rank & 127)
        base = donor[:, here]
        plane = base >> 14
        offset = jnp.where(plane == 1, offsets[0], jnp.where(plane == 2, offsets[1], jnp.where(plane == 3, offsets[2], offsets[3])))
        chosen = high_rows == offset + (spot >> 8)
        fields = [(base >> 7) & 127, base & 127, dest[:, here], rank + 1]
        fields = [field.astype(f32) for field in fields]
        for k in range(3):
            rest = fractions[k, :, here]
            for _ in range(3):
                part = rest.astype(bf16).astype(f32)
                fields.append(part)
                rest = rest - part
        spread = jnp.concatenate([jnp.where(chosen, field, 0.0) for field in fields] + [blank], axis=0)
        spreads.append(spread.astype(bf16))
        places.append(exact(low_rows == (spot & 255)))
        held = slots == rank
        mark = [jnp.where(held, part.astype(f32), 0.0) for part in ((label + 1) >> 8, (label + 1) & 255)]
        marks.append(jnp.concatenate(mark, axis=0).astype(bf16))
        targets.append(exact(inside[:128]))

    def gathered(left, right):
        left, right = jnp.concatenate(left, axis=1), jnp.concatenate(right, axis=1)
        return lax.dot_general(left, right, NT, preferred_element_type=f32)

    both = gathered(targets, marks) * jnp.where(iota((128, 128), 1) < 64, 256.0, 1.0)
    labels[...] = both + pltpu.roll(both, 64, 1)
    total = gathered(spreads, places)

    def field(i):
        return total[i * DONOR_ROWS : (i + 1) * DONOR_ROWS]

    for i in range(4):
        table[i] = field(i)
    for i in range(3):
        table[4 + i] = field(4 + 3 * i) + field(5 + 3 * i) + field(6 + 3 * i)


def prepare(donor, fractions, dest, recept):
    return pl.pallas_call(
        prepare_kernel,
        out_shape=(
            jax.ShapeDtypeStruct((7, DONOR_ROWS, TILE), f32),
            jax.ShapeDtypeStruct((128, 128), f32),
            jax.ShapeDtypeStruct((4,), i32),
        ),
        in_specs=placed("vvvv"),
        out_specs=tuple(placed("vvs")),
        compiler_params=params(),
        cost_estimate=pl.CostEstimate(flops=3 * 10**9, bytes_accessed=10**6, transcendentals=0),
    )(donor, fractions, dest, recept)


def pack_kernel(with_labels, fetched, below, beyond, table, starts, *rest):
    del below
    if with_labels:
        labels, out, source, total, state, sems = rest
    else:
        out, source, total, state, sems = rest
    copies = [pltpu.make_async_copy(fetched.at[c], state.at[c], sems.at[c]) for c in range(4)]
    for copy in copies:
        copy.start()
    inner = lax.axis_index("blk") < lax.axis_size("blk") - 1
    for c in range(4):
        copies[c].wait()
        rows = slice(c * 128, c * 128 + 128)
        for x in range(5):
            high, low = two_parts(state[c, x] if x < 4 else jnp.where(inner, beyond[c], 0.0))
            for pair, side in ((x, 0), (x - 1, 128)):
                if 0 <= pair < 4:
                    for begin, part in ((0, high), (256, low), (512, high)):
                        source[pair, rows, begin + side : begin + side + 128] = part
    total[...] = jnp.zeros_like(total)
    cells = iota((128, TILE), 0)
    slots = iota((64, TILE), 0)
    begin = tuple(starts[i] for i in range(4))

    def interpolated(t):
        line, point, target, rank, fx, fy, fz = (table[i, pl.ds(t, 1), :] for i in range(7))
        line, point, target, rank = (v.astype(i32) for v in (line, point, target, rank))
        wy = jnp.where(cells == line, 1.0 - fy, jnp.where(cells == line + 1, fy, 0.0))
        wz = jnp.where(cells == point, 1.0 - fz, jnp.where(cells == point + 1, fz, 0.0))
        first, second = two_parts(wz * (1.0 - fx)), two_parts(wz * fx)
        high = [first[0], second[0]]
        weights = jnp.concatenate(high + high + [first[1], second[1]], axis=0)
        lines = jnp.dot(source[bucket_of(t, begin)], weights, preferred_element_type=f32)
        chosen = slots == rank - 1
        values = [jnp.sum(lines[c * 128 : c * 128 + 128] * wy, axis=0, keepdims=True) for c in range(4)]
        parts = []
        for which in (0, 1):
            for c in range(4):
                part = two_parts(values[c])[which].astype(f32)
                parts.append(jnp.where(chosen, part, 0.0).astype(bf16))
        return exact(cells == target), jnp.concatenate(parts, axis=0)

    def step(t, _):
        members, packed = zip(*[interpolated(t * GROUP + j) for j in range(GROUP)])
        members, packed = jnp.concatenate(members, axis=1), jnp.concatenate(packed, axis=1)
        total[...] += lax.dot_general(members, packed, NT, preferred_element_type=f32)
        return 0

    lax.fori_loop(0, (begin[3] + GROUP - 1) // GROUP, step, 0)
    for half in range(2):
        cut = slice(half * 128, half * 128 + 128)
        low = slice(256 + half * 128, 256 + half * 128 + 128)
        out[:, half, :] = total[:, cut] + total[:, low]
    if with_labels:
        out[:, 2, :] = labels[...]
        out[:, 3, :] = jnp.zeros((128, 128), f32)


def pack(state, below, beyond, table, starts, labels=None):
    first = labels is not None
    operands = (state, below, beyond, table, starts) + ((labels,) if first else ())
    return pl.pallas_call(
        functools.partial(pack_kernel, first),
        out_shape=jax.ShapeDtypeStruct((128, 4 if first else 2, 128), f32),
        in_specs=placed("hhvvsv"[: len(operands)]),
        out_specs=placed("v")[0],
        scratch_shapes=[
            pltpu.VMEM((4, 512, 768), bf16),
            pltpu.VMEM((128, 512), f32),
            pltpu.VMEM(state.shape, f32),
            pltpu.SemaphoreType.DMA((4,)),
        ],
        compiler_params=params(),
    )(*operands)


def rates_of(x, state, below, beyond, metric, damping):
    row = iota((128, 128), 0)
    lane = iota((128, 128), 1)

    block = lax.axis_index("blk")
    inner = block > 0, block < lax.axis_size("blk") - 1

    def differences(c):
        here = state[c, x]
        low = jnp.where(inner[0], below[c], 0.0) if x == 0 else state[c, x - 1]
        high = jnp.where(inner[1], beyond[c], 0.0) if x == 3 else state[c, x + 1]
        up = jnp.where(row < 127, pltpu.roll(here, 127, 0), 0.0)
        down = jnp.where(row > 0, pltpu.roll(here, 1, 0), 0.0)
        right = jnp.where(lane < 127, pltpu.roll(here, 127, 1), 0.0)
        left = jnp.where(lane > 0, pltpu.roll(here, 1, 1), 0.0)
        return (high - low) * 0.5, (up - down) * 0.5, (right - left) * 0.5

    def gradient(diffs, i):
        return metric[i, x] * diffs[0] + metric[3 + i, x] * diffs[1] + metric[6 + i, x] * diffs[2]

    damp = damping[x]
    pressure = -damp * state[0, x]
    for i in range(3):
        pressure = pressure - gradient(differences(1 + i), i)
    diffs = differences(0)
    return [pressure] + [-gradient(diffs, i) - damp * state[1 + i, x] for i in range(3)]


def deposit_kernel(first, *refs):
    arrived, refs = refs[0], refs[1:]
    fetched, refs = refs[:5], refs[5:]
    if first:
        low_plane, high_plane, section, counts, base, cells, bounds, *scratch = refs
    else:
        counts, base, cells, bounds, out, *scratch = refs
    slots, total, count, now, below, beyond, metric, damping, sems = scratch
    held = (now, below, beyond, metric, damping)
    copies = [pltpu.make_async_copy(fetched[i], held[i], sems.at[i]) for i in range(5)]
    for copy in copies:
        copy.start()
    for j in range(2):
        turned = arrived[:, j, :].T
        for half in range(2):
            high, low = two_parts(turned[half * 64 : half * 64 + 64])
            slots[2 * j + half] = high.astype(f32)
            slots[4 + 2 * j + half] = low.astype(f32)
    if first:
        label = arrived[:, 2, :].T[:64].astype(i32) - 1
        cells[0] = (label >> 7) & 127
        cells[1] = (label >> 14) * 128 + (label & 127)
        rank = iota((64, 128), 0)
        front = (label >= 0) & (label < 32768)
        bounds[0] = (jnp.max(jnp.where(front, rank + 1, 0).astype(f32)).astype(i32) + RANKS - 1) // RANKS
        bounds[1] = jnp.min(jnp.where(label >= 32768, rank, 64).astype(f32)).astype(i32) // RANKS
        count[...] = jnp.zeros_like(count)
    total[...] = jnp.zeros_like(total)
    lines = iota((128, 128), 0)
    points = iota((256, 128), 0)

    def add(pairs, t, _):
        high, low, ones, selectors = [], [], [], []
        for j in range(RANKS):
            row = pl.ds(t * RANKS + j, 1)
            at = lines == cells[0, row, :]

            def spread(f):
                return jnp.where(at, slots[f, row, :], 0.0).astype(bf16)

            high.append(jnp.concatenate([spread(f) for f in range(4)], axis=0))
            low.append(jnp.concatenate([spread(4 + f) for f in range(4)], axis=0))
            ones.append(exact(at))
            point = cells[1, row, :]
            selectors.append(jnp.concatenate([exact(points == point - 256 * p) for p in pairs], axis=0))
        selector = jnp.concatenate(selectors + selectors, axis=1)
        added = lax.dot_general(jnp.concatenate(high + low, axis=1), selector, NT, preferred_element_type=f32)
        for i, p in enumerate(pairs):
            total[p] += added[:, i * 256 : i * 256 + 256]
        if first:
            selector = jnp.concatenate(selectors, axis=1)
            added = lax.dot_general(jnp.concatenate(ones, axis=1), selector, NT, preferred_element_type=f32)
            for i, p in enumerate(pairs):
                count[p] += added[:, i * 256 : i * 256 + 256]
        return 0

    front, back = bounds[0], bounds[1]
    lower, upper = jnp.minimum(front, back), jnp.maximum(front, back)
    lax.fori_loop(0, lower, functools.partial(add, (0,)), 0)
    lax.fori_loop(lower, front, functools.partial(add, (0, 1)), 0)
    lax.fori_loop(upper, 64 // RANKS, functools.partial(add, (1,)), 0)
    for copy in copies:
        copy.wait()
    for x in range(4):
        lanes = slice((x % 2) * 128, (x % 2) * 128 + 128)
        if first:
            counts[x] = count[x // 2, :, lanes]
        rates = rates_of(x, now, below, beyond, metric, damping)
        for c in range(4):
            fringe = total[x // 2, c * 128 : c * 128 + 128, lanes]
            rate = rates[c] + fringe - counts[x] * now[c, x]
            if first:
                section[c, x] = now[c, x] + step_size * rate
                if x in (0, 3):
                    (low_plane if x == 0 else high_plane)[c] = section[c, x]
                base[c, x] = now[c, x] + (0.5 * step_size) * rate
            else:
                out[c, x] = base[c, x] + (0.5 * step_size) * rate


def deposit(first, arrived, *operands):
    fetched = operands[:5]
    shape = fetched[0].shape
    if first:
        results = (
            jax.ShapeDtypeStruct((4, 128, 128), f32),
            jax.ShapeDtypeStruct((4, 128, 128), f32),
            jax.ShapeDtypeStruct(shape, f32),
            jax.ShapeDtypeStruct(shape[1:], f32),
            jax.ShapeDtypeStruct(shape, f32),
            jax.ShapeDtypeStruct((2, 64, 128), i32),
            jax.ShapeDtypeStruct((2,), i32),
        )
        specs, result_specs = placed("vhhhhh"), tuple(placed("vvvvvvs"))
    else:
        results, result_specs = jax.ShapeDtypeStruct(shape, f32), placed("v")[0]
        specs = placed("vhhhhhvvvs")
    return pl.pallas_call(
        functools.partial(deposit_kernel, first),
        out_shape=results,
        in_specs=specs,
        out_specs=result_specs,
        scratch_shapes=[
            pltpu.VMEM((8, 64, 128), f32),
            pltpu.VMEM((2, 512, 256), f32),
            pltpu.VMEM((2, 128, 256), f32),
        ]
        + [pltpu.VMEM(operand.shape, f32) for operand in fetched]
        + [pltpu.SemaphoreType.DMA((5,))],
        compiler_params=params(),
    )(arrived, *operands)


def neighbours(low_plane, high_plane):
    count = lax.axis_size("blk")
    forward = [(i, (i + 1) % count) for i in range(count)]
    backward = [((i + 1) % count, i) for i in range(count)]
    beyond = lax.ppermute(low_plane, "blk", backward)
    below = lax.ppermute(high_plane, "blk", forward)
    return below, beyond


def exchange(outgoing):
    return lax.all_to_all(outgoing, ("grid", "blk"), split_axis=0, concat_axis=0, tiled=True)


def local(state, metric, damping, donor, fractions, dest, recept):
    state, metric, damping = state[0], metric[0], damping[0]
    fractions = fractions.reshape(3, 1, -1)
    dest = dest.reshape(1, -1)
    below, beyond = neighbours(state[:, 0], state[:, 3])
    table, labels, tiles = prepare(donor, fractions, dest, recept)
    arrived = exchange(pack(state, below, beyond, table, tiles, labels))
    low_plane, high_plane, section, *kept = deposit(True, arrived, state, below, beyond, metric, damping)
    below, beyond = neighbours(low_plane, high_plane)
    arrived = exchange(pack(section, below, beyond, table, tiles))
    return deposit(False, arrived, section, below, beyond, metric, damping, *kept)[None]


def solution(mesh):
    in_specs = (
        P("grid", None, "blk", None, None),
        P("grid", None, "blk", None, None),
        P("grid", "blk", None, None),
        P("grid", "blk"),
        P("grid", None, "blk"),
        P("grid", "blk", None),
        P("grid", "blk"),
    )
    out_specs = P("grid", None, "blk", None, None)
    return jax.shard_map(local, mesh=mesh, in_specs=in_specs, out_specs=out_specs, check_vma=False)
```

time: 105 us -> 94 us (0.90)
  the two profiles are of different devices: /device:TPU:0 before, /device:TPU:1 now
where the time goes in v3:
time: 94 us; the launch traced here: 93.6 us
  blocking collectives  40.6 us (43%)
  Pallas kernels  39.3 us (42%)
  waiting for transfers between devices  8.58 us (9%)
  starting transfers between devices  3.41 us (4%)
  local copies, waits for them, and re-layouts  1.44 us (2%)
    all_to_all x2, blocking collectives, exchange(): lax.all_to_all(outgoing, ('grid', 'blk'), split_axis=0, concat_axis=0, ti...  40.6 us
    pallas_call x2, Pallas kernels, deposit(): pl.pallas_call(functools.partial(deposit_kernel, first), out_shape=result...  21.6 us
    pallas_call x2, Pallas kernels, pack(): pl.pallas_call(functools.partial(pack_kernel, first), out_shape=jax.Shape...  14.9 us
    ppermute x2, waiting for transfers between devices, neighbours(): below = lax.ppermute(high_plane, 'blk', forward)  4.53 us
    ppermute x2, waiting for transfers between devices, neighbours(): beyond = lax.ppermute(low_plane, 'blk', backward)  4.06 us
    pallas_call x1, Pallas kernels, prepare(): pl.pallas_call(prepare_kernel, out_shape=(jax.ShapeDtypeStruct((7, DONOR_...  2.71 us
    ppermute x2, starting transfers between devices, neighbours(): beyond = lax.ppermute(low_plane, 'blk', backward)  1.95 us
  transfers between devices with their start and end apart: 4, of which 4 were waited for; matrix products, arithmetic and copies ran while one was open for 0% of the time, Pallas kernels for 3%

profile of v3, /device:TPU:1, one launch (start us, length us, event | category | flops | bytes accessed | tf_op | source)
XLA Modules:
  0.0 93.6 jit_solution(4055732584448090973)
XLA Ops:
  0.0 0.0 copy-start.6
  0.0 0.0 copy-start.5
  0.0 0.0 copy-start.3
  0.0 0.0 copy-start.4
  0.0 1.4 %copy.13 = f32[1,4,4,128,128]{4,3,1,2,0:T(8,128)S(1)} copy(f32[1,4,4,128,128]{4,3,2,1,0:T(8,128)} %param.7) | data formatting | bytes 2097152 | tf_op args[0]
  1.4 1.5 %collective-permute-start.1 = (f32[4,128,128]{2,1,0:T(8,128)S(1)}, f32[4,128,128]{2,1,0:T(8,128)S(1)}, u32[]{:S(2)}, u32[]{:S(2)}) collective-permute-start(f32[4,128,128]{2,1,0:T(8,128)S(1)} %get-tuple-element.25), channel_id=1, source_target_pairs={{1,0},{2,1},{3,2},{4,3},{5,4},{6,5},{7,6},{8,7},{9,8},{10,9},{11,1... | collective-permute-start | bytes 786440 | tf_op jit(solution)/shard_map/ppermute | solution.py:360
  2.9 1.4 %collective-permute-start = (f32[4,128,128]{2,1,0:T(8,128)S(1)}, f32[4,128,128]{2,1,0:T(8,128)S(1)}, u32[]{:S(2)}, u32[]{:S(2)}) collective-permute-start(f32[4,128,128]{2,1,0:T(8,128)S(1)} %get-tuple-element.26), channel_id=1, source_target_pairs={{0,1},{1,2},{2,3},{3,4},{4,5},{5,6},{6,7},{7,8},{8,9},{9,10},{10,1... | collective-permute-start | bytes 786440 | tf_op jit(solution)/shard_map/ppermute | solution.py:361
  4.3 0.0 copy-done.6
  4.3 0.0 copy-done.5
  4.3 0.0 copy-done.3
  4.3 0.0 copy-done.4
  4.3 0.0 copy-start
  4.3 0.0 copy-start.2
  4.3 2.7 %shard_map.73 = (f32[7,24,256]{2,1,0:T(8,128)S(1)}, f32[128,128]{1,0:T(8,128)S(1)}, s32[4]{0:T(128)S(1)}) custom-call(s32[1,4096]{1,0:T(1,128)S(1)} %copy-done.4, f32[3,1,4096]{2,1,0:T(1,128)S(1)} %bitcast.19, s32[1,4096]{1,0:T(1,128)S(1)} %bitcast.20, s32[1,4096]{1,0:T(1,128)S(1)} %copy-done.6), custom_call_target="tpu_custom_call" | custom-call | flops 3000000000 | bytes 1000000 | tf_op jit(solution)/shard_map/pallas_call | solution.py:125
  7.0 0.0 copy-start.1
  7.0 1.2 %collective-permute-done.1.beyond.refs_3_ = f32[4,128,128]{2,1,0:T(8,128)S(1)} collective-permute-done((f32[4,128,128]{2,1,0:T(8,128)S(1)}, f32[4,128,128]{2,1,0:T(8,128)S(1)}, u32[]{:S(2)}, u32[]{:S(2)}) %collective-permute-start.1) | collective-permute-done | bytes 262176 | tf_op jit(solution)/shard_map/ppermute | solution.py:360
  8.3 1.7 %collective-permute-done.below.refs_2_ = f32[4,128,128]{2,1,0:T(8,128)S(1)} collective-permute-done((f32[4,128,128]{2,1,0:T(8,128)S(1)}, f32[4,128,128]{2,1,0:T(8,128)S(1)}, u32[]{:S(2)}, u32[]{:S(2)}) %collective-permute-start) | collective-permute-done | bytes 262176 | tf_op jit(solution)/shard_map/ppermute | solution.py:361
  10.0 0.0 copy-done
  10.0 7.5 %shard_map.74 = f32[128,4,128]{2,1,0:T(4,128)S(1)} custom-call(f32[4,4,128,128]{3,2,1,0:T(8,128)S(1)} %bitcast.13, f32[4,128,128]{2,1,0:T(8,128)S(1)} %collective-permute-done.below.refs_2_, f32[4,128,128]{2,1,0:T(8,128)S(1)} %collective-permute-done.1.beyond.refs_3_, f32[7,24,256]{2,1,0:T(8,128)S(1)} %get-tuple-element.15.table, ...), custom_call_target="tpu_custom_call" | custom-call | tf_op jit(solution)/shard_map/pallas_call | solution.py:200
  17.5 22.7 %all_to_all.10.refs_0_ = f32[128,4,128]{2,1,0:T(4,128)S(1)} all-to-all(f32[128,4,128]{2,1,0:T(4,128)S(1)} %shard_map.74), channel_id=1, replica_groups=mesh['grid'=4,'blk'=32] {'grid','blk'}, dimensions={0} | all-to-all | bytes 524288 | tf_op jit(solution)/shard_map/all_to_all | solution.py:366
  40.2 0.0 copy-done.2
  40.2 0.0 copy-done.1
  40.2 11.1 %shard_map.75 = (f32[4,128,128]{2,1,0:T(8,128)S(1)}, f32[4,128,128]{2,1,0:T(8,128)S(1)}, f32[4,4,128,128]{3,2,1,0:T(8,128)S(1)}, f32[4,128,128]{2,1,0:T(8,128)S(...) custom-call(f32[128,4,128]{2,1,0:T(4,128)S(1)} %all_to_all.10.refs_0_, ...), custom_call_target="tpu_custom_call" | custom-call | tf_op jit(solution)/shard_map/pallas_call | solution.py:340
  51.3 0.1 collective-permute-start.2
  51.4 0.5 collective-permute-start.3
  51.9 2.8 %collective-permute-done.2.below.refs_2_ = f32[4,128,128]{2,1,0:T(8,128)S(1)} collective-permute-done((f32[4,128,128]{2,1,0:T(8,128)S(1)}, f32[4,128,128]{2,1,0:T(8,128)S(1)}, u32[]{:S(2)}, u32[]{:S(2)}) %collective-permute-start.2) | collective-permute-done | bytes 262176 | tf_op jit(solution)/shard_map/ppermute | solution.py:361
  54.7 2.9 %collective-permute-done.3.beyond.refs_3_ = f32[4,128,128]{2,1,0:T(8,128)S(1)} collective-permute-done((f32[4,128,128]{2,1,0:T(8,128)S(1)}, f32[4,128,128]{2,1,0:T(8,128)S(1)}, u32[]{:S(2)}, u32[]{:S(2)}) %collective-permute-start.3) | collective-permute-done | bytes 262176 | tf_op jit(solution)/shard_map/ppermute | solution.py:360
  57.6 7.4 %shard_map.76 = f32[128,2,128]{2,1,0:T(2,128)S(1)} custom-call(f32[4,4,128,128]{3,2,1,0:T(8,128)S(1)} %get-tuple-element.18.fetched.refs_1_, f32[4,128,128]{2,1,0:T(8,128)S(1)} %collective-permute-done.2.below.refs_2_, f32[4,128,128]{2,1,0:T(8,128)S(1)} %collective-permute-done.3.beyond.refs_3_, f32[7,24,256]{2,1,0:T(8,128)S(1)} %get-tuple-element.15.table, ...), custom_call_target="tpu_custom_call" | custom-call | tf_op jit(solution)/shard_map/pallas_call | solution.py:200
  65.0 18.0 %all_to_all.11.refs_0_ = f32[128,2,128]{2,1,0:T(2,128)S(1)} all-to-all(f32[128,2,128]{2,1,0:T(2,128)S(1)} %shard_map.76), channel_id=1, replica_groups=mesh['grid'=4,'blk'=32] {'grid','blk'}, dimensions={0} | all-to-all | bytes 262144 | tf_op jit(solution)/shard_map/all_to_all | solution.py:366
  83.0 10.5 %shard_map.77 = f32[4,4,128,128]{3,2,1,0:T(8,128)} custom-call(f32[128,2,128]{2,1,0:T(2,128)S(1)} %all_to_all.11.refs_0_, f32[4,4,128,128]{3,2,1,0:T(8,128)S(1)} %get-tuple-element.18.fetched.refs_1_, f32[4,128,128]{2,1,0:T(8,128)S(1)} %collective-permute-done.2.below.refs_2_, f32[4,128,128]{2,1,0:T(8,128)S(1)} %collective-permute-done.3.beyond.refs_3_, ...), custom_call_target="tpu_custom_call" | custom-call | tf_op jit(solution)/shard_map/pallas_call | solution.py:340
  (1 shorter events, 0.0 us)
Async XLA Ops:
  0.0 4.3 %copy-start.6 = (s32[1,4096]{1,0:T(1,128)S(1)}, s32[1,4096]{1,0:T(1,128)}, u32[]{:S(2)}) copy-start(s32[1,4096]{1,0:T(1,128)} %recept.1) | copy-start | bytes 49156
  0.0 4.3 %copy-start.5 = (s32[1,4096,1]{1,2,0:T(1,128)S(1)}, s32[1,4096,1]{1,2,0:T(1,128)}, u32[]{:S(2)}) copy-start(s32[1,4096,1]{1,2,0:T(1,128)} %param.12) | copy-start | bytes 49156
  0.0 4.3 %copy-start.3 = (f32[1,3,4096]{2,0,1:T(1,128)S(1)}, f32[1,3,4096]{2,0,1:T(1,128)}, u32[]{:S(2)}) copy-start(f32[1,3,4096]{2,0,1:T(1,128)} %param.11) | copy-start | bytes 147460
  0.0 4.3 %copy-start.4 = (s32[1,4096]{1,0:T(1,128)S(1)}, s32[1,4096]{1,0:T(1,128)}, u32[]{:S(2)}) copy-start(s32[1,4096]{1,0:T(1,128)} %donor.1) | copy-start | bytes 49156
  1.4 6.8 %collective-permute-start.1 = (f32[4,128,128]{2,1,0:T(8,128)S(1)}, f32[4,128,128]{2,1,0:T(8,128)S(1)}, u32[]{:S(2)}, u32[]{:S(2)}) collective-permute-start(f32[4,128,128]{2,1,0:T(8,128)S(1)} %get-tuple-element.25), channel_id=1, source_target_pairs={{1,0},{2,1},{3,2},{4,3},{5,4},{6,5},{7,6},{8,7},{9,8},{10,9},{11,1... | collective-permute-start | bytes 786440 | tf_op jit(solution)/shard_map/ppermute | solution.py:360
  2.9 7.1 %collective-permute-start = (f32[4,128,128]{2,1,0:T(8,128)S(1)}, f32[4,128,128]{2,1,0:T(8,128)S(1)}, u32[]{:S(2)}, u32[]{:S(2)}) collective-permute-start(f32[4,128,128]{2,1,0:T(8,128)S(1)} %get-tuple-element.26), channel_id=1, source_target_pairs={{0,1},{1,2},{2,3},{3,4},{4,5},{5,6},{6,7},{7,8},{8,9},{9,10},{10,1... | collective-permute-start | bytes 786440 | tf_op jit(solution)/shard_map/ppermute | solution.py:361
  4.3 5.7 %copy-start = (f32[1,4,4,128,128]{4,3,2,1,0:T(8,128)S(1)}, f32[1,4,4,128,128]{4,3,2,1,0:T(8,128)}, u32[]{:S(2)}) copy-start(f32[1,4,4,128,128]{4,3,2,1,0:T(8,128)} %param.7) | copy-start | bytes 3145732
  4.3 35.9 %copy-start.2 = (f32[1,4,128,128]{3,2,1,0:T(8,128)S(1)}, f32[1,4,128,128]{3,2,1,0:T(8,128)}, u32[]{:S(2)}) copy-start(f32[1,4,128,128]{3,2,1,0:T(8,128)} %param.9) | copy-start | bytes 786436
  7.0 33.1 %copy-start.1 = (f32[1,9,4,128,128]{4,3,2,1,0:T(8,128)S(1)}, f32[1,9,4,128,128]{4,3,2,1,0:T(8,128)}, u32[]{:S(2)}) copy-start(f32[1,9,4,128,128]{4,3,2,1,0:T(8,128)} %param.8) | copy-start | bytes 7077892
  51.3 3.4 %collective-permute-start.2 = (f32[4,128,128]{2,1,0:T(8,128)S(1)}, f32[4,128,128]{2,1,0:T(8,128)S(1)}, u32[]{:S(2)}, u32[]{:S(2)}) collective-permute-start(f32[4,128,128]{2,1,0:T(8,128)S(1)} %get-tuple-element.19), channel_id=1, source_target_pairs={{0,1},{1,2},{2,3},{3,4},{4,5},{5,6},{6,7},{7,8},{8,9},{9,10},{10,1... | collective-permute-start | bytes 786440 | tf_op jit(solution)/shard_map/ppermute | solution.py:361
  51.4 6.2 %collective-permute-start.3 = (f32[4,128,128]{2,1,0:T(8,128)S(1)}, f32[4,128,128]{2,1,0:T(8,128)S(1)}, u32[]{:S(2)}, u32[]{:S(2)}) collective-permute-start(f32[4,128,128]{2,1,0:T(8,128)S(1)} %get-tuple-element.20), channel_id=1, source_target_pairs={{1,0},{2,1},{3,2},{4,3},{5,4},{6,5},{7,6},{8,7},{9,8},{10,9},{11,1... | collective-permute-start | bytes 786440 | tf_op jit(solution)/shard_map/ppermute | solution.py:360
